TPU v7x, 32 devices: a whole 2x2x4 slice. The times are simulated.
32 devices in a mesh: fsdp: 2 (over y), context: 4 (over z), tensor: 4 (over x, core).
Axes of the slice: x: 2, y: 2, z: 4, core: 2. Of those that a mesh axis runs over, the one named last changes fastest.
Arguments:
- tokens: bfloat16 [2, 1088, 1024], P('fsdp', 'context'), may hold values from -6 to 6
- segments: int32 [2, 1088], P('fsdp', 'context'), may hold values from 0 to 3, as said below
- cotangent: bfloat16 [2, 1088, 1024], P('fsdp', 'context'), may hold values from -6 to 6
- w_qkv: bfloat16 [1024, 3, 1024], P('fsdp', None, 'tensor'), may hold values from -0.1875 to 0.1875
- b_qv: bfloat16 [2, 16, 64], P(None, 'tensor', 'fsdp'), may hold values from -1.5 to 1.5
- w_out: bfloat16 [1024, 1024], P('tensor', 'fsdp'), may hold values from -1.5 to 1.5
- b_out: bfloat16 [1024], P('fsdp'), may hold values from -1.5 to 1.5
- w_fc: bfloat16 [1024, 4096], P('fsdp', 'tensor'), may hold values from -0.1875 to 0.1875
- b_fc: bfloat16 [16, 256], P('tensor', 'fsdp'), may hold values from -1.5 to 1.5
- w_proj: bfloat16 [4096, 1024], P('tensor', 'fsdp'), may hold values from -0.09375 to 0.09375
- b_proj: bfloat16 [1024], P('fsdp'), may hold values from -1.5 to 1.5
- ln1_gain: bfloat16 [1024], P('fsdp'), may hold values from 0.25 to 1.75
- ln1_shift: bfloat16 [1024], P('fsdp'), may hold values from -1.5 to 1.5
- ln2_gain: bfloat16 [1024], P('fsdp'), may hold values from 0.25 to 1.75
- ln2_shift: bfloat16 [1024], P('fsdp'), may hold values from -1.5 to 1.5
Outputs:
- mixed: bfloat16 [2, 1088, 1024], P('fsdp', 'context')
- grad_tokens: float32 [2, 1088, 1024], P('fsdp', 'context')
- grad_w_qkv: float32 [1024, 3, 1024], P('fsdp', None, 'tensor')
- grad_b_qv: float32 [2, 16, 64], P(None, 'tensor', 'fsdp')
- grad_w_out: float32 [1024, 1024], P('tensor', 'fsdp')
- grad_b_out: float32 [1024], P('fsdp')
- grad_w_fc: float32 [1024, 4096], P('fsdp', 'tensor')
- grad_b_fc: float32 [16, 256], P('tensor', 'fsdp')
- grad_w_proj: float32 [4096, 1024], P('tensor', 'fsdp')
- grad_b_proj: float32 [1024], P('fsdp')
- grad_ln1_gain: float32 [1024], P('fsdp')
- grad_ln1_shift: float32 [1024], P('fsdp')
- grad_ln2_gain: float32 [1024], P('fsdp')
- grad_ln2_shift: float32 [1024], P('fsdp')
Inputs may be any that keep to these rules, and one draw needn't show every extreme that they name: `segments`: in each of the 2 rows the sequence numbers run 0, 1, 2, 3 in order, each present; sequence 1 has exactly 1024 positions and starts within the first 272 positions of its row.
All inputs are finite; a program needn't handle non-finite values.
Results may differ from a plain program's by a relative error of at most 0.017.
Values may be sent and summed in bfloat16 or wider, within the bound.
A program may use at most 128 MiB of HBM per device.

v0:
```python
import jax
import jax.numpy as jnp
from jax import lax
from jax.sharding import PartitionSpec as P

HD = 64


EPSILON = 1e-05
MASK_FILL = 1e30
SCORE_SCALE = 0.125


def layer_norm(values, gain, shift):
    mean = jnp.mean(values, axis=-1, keepdims=True)
    centred = values - mean
    spread = jnp.mean(centred * centred, axis=-1, keepdims=True)
    return centred * lax.rsqrt(spread + EPSILON) * gain + shift


def gelu_tanh(values):
    inner = 0.7978845608028654 * (values + 0.044715 * values * values * values)
    return 0.5 * values * (1.0 + jnp.tanh(inner))


def visible(segments, key_segments, first_row):
    row_count = segments.shape[1]
    query_pos = first_row + jnp.arange(row_count, dtype=jnp.int32)
    key_pos = jnp.arange(key_segments.shape[1], dtype=jnp.int32)
    same = segments.astype(jnp.float32)[:, :, None] == key_segments.astype(jnp.float32)[:, None, :]
    return same & (key_pos[None, None, :] <= query_pos[None, :, None])


def scores_of(queries, keys_all, key_mask):
    raw_scores = jnp.einsum(
        "pqhe,pkhe->phqk", queries, keys_all, preferred_element_type=jnp.float32
    )
    return jnp.where(key_mask[:, None], SCORE_SCALE * raw_scores, -MASK_FILL)


def body(
    tokens,
    segments,
    cotangent,
    w_qkv,
    b_qv,
    w_out,
    b_out,
    w_fc,
    b_fc,
    w_proj,
    b_proj,
    ln1_gain,
    ln1_shift,
    ln2_gain,
    ln2_shift,
):
    pack_count, row_count, model_width = tokens.shape
    head_count = b_qv.shape[1]
    local_width = head_count * HD
    gathered = (
        lax.all_gather(w_qkv, "fsdp", axis=0, tiled=True),
        lax.all_gather(w_out, "fsdp", axis=1, tiled=True),
        lax.all_gather(w_fc, "fsdp", axis=0, tiled=True),
        lax.all_gather(w_proj, "fsdp", axis=1, tiled=True),
        lax.all_gather(b_qv, "fsdp", axis=2, tiled=True),
        lax.all_gather(b_out, "fsdp", axis=0, tiled=True),
        lax.all_gather(b_fc, "fsdp", axis=1, tiled=True),
        lax.all_gather(b_proj, "fsdp", axis=0, tiled=True),
        lax.all_gather(ln1_gain, "fsdp", axis=0, tiled=True),
        lax.all_gather(ln1_shift, "fsdp", axis=0, tiled=True),
        lax.all_gather(ln2_gain, "fsdp", axis=0, tiled=True),
        lax.all_gather(ln2_shift, "fsdp", axis=0, tiled=True),
    )
    qkv_all = gathered[0]
    out_all = gathered[1]
    fc_all = gathered[2]
    proj_all = gathered[3]
    bias_qv = gathered[4].astype(jnp.float32).reshape(2, local_width)
    bias_out = gathered[5].astype(jnp.float32)
    bias_fc = gathered[6].astype(jnp.float32).reshape(-1)
    bias_proj = gathered[7].astype(jnp.float32)
    gain_one = gathered[8].astype(jnp.float32)
    shift_one = gathered[9].astype(jnp.float32)
    gain_two = gathered[10].astype(jnp.float32)
    shift_two = gathered[11].astype(jnp.float32)
    first_row = lax.axis_index("context") * row_count
    base_rows = tokens.astype(jnp.float32)
    normed1 = layer_norm(base_rows, gain_one, shift_one).astype(jnp.bfloat16)
    projected = jnp.einsum("ptd,dje->ptje", normed1, qkv_all, preferred_element_type=jnp.float32)
    queries_low = (projected[:, :, 0] + bias_qv[0]).astype(jnp.bfloat16)
    keys_low = projected[:, :, 1].astype(jnp.bfloat16)
    values_low = (projected[:, :, 2] + bias_qv[1]).astype(jnp.bfloat16)
    seg_low = segments.astype(jnp.bfloat16)
    fetched = (
        lax.all_gather(keys_low, "context", axis=1, tiled=True),
        lax.all_gather(values_low, "context", axis=1, tiled=True),
        lax.all_gather(seg_low, "context", axis=1, tiled=True),
    )
    keys_all = fetched[0].reshape(pack_count, -1, head_count, HD)
    values_all = fetched[1].reshape(pack_count, -1, head_count, HD)
    key_mask = visible(segments, fetched[2], first_row)
    queries = queries_low.reshape(pack_count, row_count, head_count, HD)
    scores = scores_of(queries, keys_all, key_mask)
    row_top = jnp.max(scores, axis=-1, keepdims=True)
    exponent = jnp.exp(scores - row_top)
    row_total = jnp.sum(exponent, axis=-1, keepdims=True)
    probs = (exponent / row_total).astype(jnp.bfloat16)
    logsum = row_top + jnp.log(row_total)
    attended = jnp.einsum("phqk,pkhe->pqhe", probs, values_all, preferred_element_type=jnp.float32)
    attended = attended.reshape(pack_count, row_count, local_width).astype(jnp.bfloat16)
    attn_part = jnp.einsum("pte,ed->ptd", attended, out_all, preferred_element_type=jnp.float32)
    hidden_state = base_rows + lax.psum(attn_part, "tensor") + bias_out
    normed2 = layer_norm(hidden_state, gain_two, shift_two).astype(jnp.bfloat16)
    pre_act = (
        jnp.einsum("ptd,df->ptf", normed2, fc_all, preferred_element_type=jnp.float32) + bias_fc
    )
    activ = gelu_tanh(pre_act).astype(jnp.bfloat16)
    mlp_part = jnp.einsum("ptf,fd->ptd", activ, proj_all, preferred_element_type=jnp.float32)
    mixed = (
        hidden_state
        + lax.psum(mlp_part.astype(jnp.bfloat16), "tensor").astype(jnp.float32)
        + bias_proj
    ).astype(jnp.bfloat16)
    grad_out = cotangent.astype(jnp.float32)
    grad_b_proj = jnp.sum(grad_out, axis=(0, 1))
    grad_w_proj = jnp.einsum("ptf,ptd->fd", activ, cotangent, preferred_element_type=jnp.float32)
    grad_activ = jnp.einsum("ptd,fd->ptf", cotangent, proj_all, preferred_element_type=jnp.float32)
    unused, gelu_pull = jax.vjp(gelu_tanh, pre_act)
    grad_pre = gelu_pull(grad_activ)[0].astype(jnp.bfloat16)
    grad_b_fc = jnp.sum(grad_pre.astype(jnp.float32), axis=(0, 1)).reshape(gathered[6].shape)
    grad_w_fc = jnp.einsum("ptd,ptf->df", normed2, grad_pre, preferred_element_type=jnp.float32)
    grad_normed2 = jnp.einsum("ptf,df->ptd", grad_pre, fc_all, preferred_element_type=jnp.float32)
    grad_normed2 = lax.psum(grad_normed2, "tensor")
    unused_two, norm_pull = jax.vjp(layer_norm, hidden_state, gain_two, shift_two)
    grad_hidden_norm, grad_gain_two, grad_shift_two = norm_pull(grad_normed2)
    grad_hidden = grad_out + grad_hidden_norm
    grad_branch = grad_hidden.astype(jnp.bfloat16)
    grad_b_out = jnp.sum(grad_hidden, axis=(0, 1))
    grad_w_out = jnp.einsum(
        "pte,ptd->ed", attended, grad_branch, preferred_element_type=jnp.float32
    )
    grad_attended = jnp.einsum(
        "ptd,ed->pte", grad_branch, out_all, preferred_element_type=jnp.float32
    )
    grad_attended = grad_attended.astype(jnp.bfloat16)
    scores = scores_of(queries, keys_all, key_mask)
    probs_full = jnp.exp(scores - logsum)
    grad_heads = grad_attended.reshape(pack_count, row_count, head_count, HD)
    grad_probs = jnp.einsum(
        "pqhe,pkhe->phqk", grad_heads, values_all, preferred_element_type=jnp.float32
    )
    row_delta = jnp.sum(grad_probs * probs_full, axis=-1, keepdims=True)
    grad_scores = (probs_full * (grad_probs - row_delta)).astype(jnp.bfloat16)
    probs_low = probs_full.astype(jnp.bfloat16)
    grad_queries = SCORE_SCALE * jnp.einsum(
        "phqk,pkhe->pqhe", grad_scores, keys_all, preferred_element_type=jnp.float32
    )
    grad_queries = grad_queries.reshape(pack_count, row_count, local_width).astype(jnp.bfloat16)
    key_count = lax.axis_size("context") * row_count
    grad_key_part = SCORE_SCALE * jnp.einsum(
        "phqk,pqhe->kphe", grad_scores, queries, preferred_element_type=jnp.float32
    )
    grad_value_part = jnp.einsum(
        "phqk,pqhe->kphe", probs_low, grad_heads, preferred_element_type=jnp.float32
    )
    summed = lax.psum_scatter(
        jnp.stack(
            (
                grad_key_part.reshape(key_count, pack_count, local_width),
                grad_value_part.reshape(key_count, pack_count, local_width),
            ),
            axis=2,
        ),
        "context",
        scatter_dimension=0,
        tiled=True,
    )
    grad_keys = summed[:, :, 0].astype(jnp.bfloat16)
    grad_values = summed[:, :, 1].astype(jnp.bfloat16)
    grad_normed1 = (
        jnp.einsum("pte,de->ptd", grad_queries, qkv_all[:, 0], preferred_element_type=jnp.float32)
        + jnp.einsum("tpe,de->ptd", grad_keys, qkv_all[:, 1], preferred_element_type=jnp.float32)
        + jnp.einsum("tpe,de->ptd", grad_values, qkv_all[:, 2], preferred_element_type=jnp.float32)
    )
    grad_normed1 = lax.psum(grad_normed1.astype(jnp.bfloat16), "tensor").astype(jnp.float32)
    grad_w_query = jnp.einsum(
        "ptd,pte->de", normed1, grad_queries, preferred_element_type=jnp.float32
    )
    grad_w_key = jnp.einsum("ptd,tpe->de", normed1, grad_keys, preferred_element_type=jnp.float32)
    grad_w_value = jnp.einsum(
        "ptd,tpe->de", normed1, grad_values, preferred_element_type=jnp.float32
    )
    grad_w_qkv = jnp.stack((grad_w_query, grad_w_key, grad_w_value), axis=1)
    grad_b_qv = jnp.stack(
        (
            jnp.sum(grad_queries.astype(jnp.float32), axis=(0, 1)),
            jnp.sum(grad_values.astype(jnp.float32), axis=(0, 1)),
        )
    ).reshape(2, head_count, HD)
    unused_one, first_pull = jax.vjp(layer_norm, base_rows, gain_one, shift_one)
    grad_base_norm, grad_gain_one, grad_shift_one = first_pull(grad_normed1)
    grad_tokens = grad_hidden + grad_base_norm
    shards = (
        lax.psum_scatter(
            grad_w_qkv.astype(jnp.bfloat16), "fsdp", scatter_dimension=0, tiled=True
        ).astype(jnp.float32),
        lax.psum_scatter(
            grad_b_qv.astype(jnp.bfloat16), "fsdp", scatter_dimension=2, tiled=True
        ).astype(jnp.float32),
        lax.psum_scatter(
            grad_w_out.astype(jnp.bfloat16), "fsdp", scatter_dimension=1, tiled=True
        ).astype(jnp.float32),
        lax.psum_scatter(
            grad_b_out.astype(jnp.bfloat16), "fsdp", scatter_dimension=0, tiled=True
        ).astype(jnp.float32),
        lax.psum_scatter(
            grad_w_fc.astype(jnp.bfloat16), "fsdp", scatter_dimension=0, tiled=True
        ).astype(jnp.float32),
        lax.psum_scatter(
            grad_b_fc.astype(jnp.bfloat16), "fsdp", scatter_dimension=1, tiled=True
        ).astype(jnp.float32),
        lax.psum_scatter(
            grad_w_proj.astype(jnp.bfloat16), "fsdp", scatter_dimension=1, tiled=True
        ).astype(jnp.float32),
        lax.psum_scatter(
            grad_b_proj.astype(jnp.bfloat16), "fsdp", scatter_dimension=0, tiled=True
        ).astype(jnp.float32),
        lax.psum_scatter(
            grad_gain_one.astype(jnp.bfloat16), "fsdp", scatter_dimension=0, tiled=True
        ).astype(jnp.float32),
        lax.psum_scatter(
            grad_shift_one.astype(jnp.bfloat16), "fsdp", scatter_dimension=0, tiled=True
        ).astype(jnp.float32),
        lax.psum_scatter(
            grad_gain_two.astype(jnp.bfloat16), "fsdp", scatter_dimension=0, tiled=True
        ).astype(jnp.float32),
        lax.psum_scatter(
            grad_shift_two.astype(jnp.bfloat16), "fsdp", scatter_dimension=0, tiled=True
        ).astype(jnp.float32),
    )
    reduced = (
        lax.psum(shards[0].astype(jnp.bfloat16), "context").astype(jnp.float32),
        lax.psum(shards[1].astype(jnp.bfloat16), "context").astype(jnp.float32),
        lax.psum(shards[2].astype(jnp.bfloat16), "context").astype(jnp.float32),
        lax.psum(shards[3].astype(jnp.bfloat16), "context").astype(jnp.float32),
        lax.psum(shards[4].astype(jnp.bfloat16), "context").astype(jnp.float32),
        lax.psum(shards[5].astype(jnp.bfloat16), "context").astype(jnp.float32),
        lax.psum(shards[6].astype(jnp.bfloat16), "context").astype(jnp.float32),
        lax.psum(shards[7].astype(jnp.bfloat16), "context").astype(jnp.float32),
        lax.psum(shards[8].astype(jnp.bfloat16), "context").astype(jnp.float32),
        lax.psum(shards[9].astype(jnp.bfloat16), "context").astype(jnp.float32),
        lax.psum(shards[10].astype(jnp.bfloat16), "context").astype(jnp.float32),
        lax.psum(shards[11].astype(jnp.bfloat16), "context").astype(jnp.float32),
    )
    return (
        mixed,
        grad_tokens,
        reduced[0],
        reduced[1],
        reduced[2],
        reduced[3],
        reduced[4],
        reduced[5],
        reduced[6],
        reduced[7],
        reduced[8],
        reduced[9],
        reduced[10],
        reduced[11],
    )


def solution(mesh):
    return jax.shard_map(
        body,
        mesh=mesh,
        in_specs=(
            P("fsdp", "context", None),
            P("fsdp", "context"),
            P("fsdp", "context", None),
            P("fsdp", None, "tensor"),
            P(None, "tensor", "fsdp"),
            P("tensor", "fsdp"),
            P("fsdp"),
            P("fsdp", "tensor"),
            P("tensor", "fsdp"),
            P("tensor", "fsdp"),
            P("fsdp"),
            P("fsdp"),
            P("fsdp"),
            P("fsdp"),
            P("fsdp"),
        ),
        out_specs=(
            P("fsdp", "context", None),
            P("fsdp", "context", None),
            P("fsdp", None, "tensor"),
            P(None, "tensor", "fsdp"),
            P("tensor", "fsdp"),
            P("fsdp"),
            P("fsdp", "tensor"),
            P("tensor", "fsdp"),
            P("tensor", "fsdp"),
            P("fsdp"),
            P("fsdp"),
            P("fsdp"),
            P("fsdp"),
            P("fsdp"),
        ),
        check_vma=False,
    )
```

profile of v0, /device:TPU:0, one launch (start us, length us, event | category | flops | bytes accessed | tf_op | source)
XLA Modules:
  0.0 667.8 jit_solution(5762590000438991754)
XLA Ops:
  8.8 5.3 all_gather.48
  15.6 4.3 all-gather.2
  20.6 4.3 all-gather.1
  26.7 12.5 %all-reduce = bf16[1088]{0:T(1024)(128)(2,1)S(1)} all-reduce(bf16[1088]{0:T(1024)(128)(2,1)S(1)} %dynamic-update-slice), channel_id=1, replica_groups=mesh['fsdp'=2,'context'=4,'tensor'=4] {'context'}, use_global_device_ids=true, to_apply=%add | all-reduce | flops 1088 | bytes 4352
  39.2 7.0 %all_gather.52 = bf16[256,1024]{1,0:T(8,128)(2,1)S(1)} all-gather(bf16[256,512]{1,0:T(8,128)(2,1)S(1)} %copy-done.24), channel_id=1, replica_groups=mesh['fsdp'=2,'context'=4,'tensor'=4] {'fsdp'}, dimensions={1}, use_global_device_ids=true | all-gather | bytes 786432 | tf_op jit(solution)/shard_map/all_gather | solution.py:63
  47.3 2.1 convolution_bitcast_fusion.5
  50.9 16.4 %all_gather.49 = bf16[1,1088,256]{2,1,0:T(8,128)(2,1)S(1)} all-gather(bf16[1,272,256]{2,1,0:T(8,128)(2,1)S(1)} %fusion.50), channel_id=1, replica_groups=mesh['fsdp'=2,'context'=4,'tensor'=4] {'context'}, dimensions={1}, use_global_device_ids=true | all-gather | bytes 696320 | tf_op jit(solution)/shard_map/all_gather | solution.py:97
  67.6 15.8 %all-gather = bf16[1,1088,1,256]{3,1,2,0:T(8,128)(2,1)S(1)} all-gather(bf16[1,272,1,256]{3,1,2,0:T(8,128)(2,1)S(1)} %copy-done.23), channel_id=2, replica_groups=mesh['fsdp'=2,'context'=4,'tensor'=4] {'context'}, dimensions={1}, use_global_device_ids=true | all-gather | bytes 696320 | tf_op jit(solution)/shard_map/all_gather | solution.py:96
  83.7 1.3 copy.51
  85.0 1.3 fusion.76
  87.3 1.3 copy-done
  88.6 1.3 fusion.22
  90.0 1.3 convolution_bitcast_fusion.4
  92.7 4.3 all-gather.3
  97.1 4.2 all_gather.57
  101.4 4.3 all-gather.5
  105.7 4.3 all-gather.4
  110.1 16.5 %all-reduce.18.cloned.1.call-done = f32[1,272,1024]{2,1,0:T(8,128)} async-done(((f32[1,272,1024]{2,1,0:T(8,128)}), f32[1,272,1024]{2,1,0:T(8,128)}) %all-reduce.18.cloned.1.call-update) | async-done | bytes 1114128 | tf_op jit(solution)/shard_map/psum | solution.py:113
  126.6 1.5 fusion.71
  128.4 33.3 %all-gather.13.cloned.1.call-done = bf16[1024,1024]{1,0:T(8,128)(2,1)} async-done(((bf16[512,1024]{1,0:T(8,128)(2,1)}), bf16[1024,1024]{1,0:T(8,128)(2,1)}) %all-gather.13.cloned.1.call-update) | async-done | bytes 2097168 | tf_op jit(solution)/shard_map/all_gather | solution.py:64
  161.6 2.4 convolution_add_fusion
  164.1 32.2 %all-gather.15.cloned.1.call-done = bf16[1024,1024]{1,0:T(8,128)(2,1)} async-done(((bf16[1024,512]{1,0:T(8,128)(2,1)}), bf16[1024,1024]{1,0:T(8,128)(2,1)}) %all-gather.15.cloned.1.call-update) | async-done | bytes 2097168 | tf_op jit(solution)/shard_map/all_gather | solution.py:65
  196.3 3.9 fusion.77
  201.0 1.8 convolution_bitcast_fusion.3
  203.7 35.9 %all-reduce.20.cloned.1.call-done = f32[1,272,1024]{2,1,0:T(8,128)} async-done(((f32[1,272,1024]{2,1,0:T(8,128)}), f32[1,272,1024]{2,1,0:T(8,128)}) %all-reduce.20.cloned.1.call-update) | async-done | bytes 1114128 | tf_op jit(solution)/shard_map/psum | solution.py:134
  239.6 2.3 multiply_reduce_fusion.1
  243.0 1.0 convolution_convert_fusion.7
  244.1 1.1 copy.54
  245.2 4.5 fusion.2
  249.7 3.9 multiply_reduce_fusion
  253.6 1.2 multiply_convert_fusion
  254.9 1.8 convolution_multiply_fusion
  256.6 1.6 bitcast_reduce_fusion
  258.2 1.3 convolution_convert_fusion.3
  259.6 3.7 copy.56
  263.3 3.7 copy.55
  266.9 4.3 pad_maximum_fusion
  271.2 82.8 %all-reduce.25 = bf16[1088,1,2,256]{3,2,1,0:T(2,128)(2,1)} all-reduce(f32[1088,1,2,256]{3,2,1,0:T(2,128)} %pad_maximum_fusion), channel_id=3, replica_groups=mesh['fsdp'=2,'context'=4,'tensor'=4] {'context'}, use_global_device_ids=true, to_apply=%region_12.13.clone | all-reduce | flops 557056 | bytes 3342336
  354.1 1.2 constant_dynamic-slice_fusion
  357.6 1.3 pad_maximum_fusion.1
  359.6 3.8 convolution_convert_fusion.1
  363.7 4.0 convolution_convert_fusion
  369.3 3.6 fusion.17
  375.0 1.5 reshape.598
  376.6 1.6 convolution_bitcast_fusion
  378.2 1.3 convolution_bitcast_fusion.1
  379.5 1.2 fusion.14
  380.8 14.7 %reduce-scatter.11.cloned.1.call-done = bf16[512,3,256]{2,0,1:T(8,128)(2,1)} async-done(((bf16[1024,3,256]{2,0,1:T(8,128)(2,1)}), bf16[512,3,256]{2,0,1:T(8,128)(2,1)}) %reduce-scatter.11.cloned.1.call-update) | async-done | bytes 786448 | tf_op jit(solution)/shard_map/reduce_scatter | solution.py:205
  395.5 34.8 %reduce-scatter.15.cloned.1.call-done = bf16[512,1024]{1,0:T(8,128)(2,1)} async-done(((bf16[1024,1024]{1,0:T(8,128)(2,1)}), bf16[512,1024]{1,0:T(8,128)(2,1)}) %reduce-scatter.15.cloned.1.call-update) | async-done | bytes 1048592 | tf_op jit(solution)/shard_map/reduce_scatter | solution.py:217
  430.3 34.8 %reduce-scatter.17.cloned.1.call-done = bf16[1024,512]{1,0:T(8,128)(2,1)} async-done(((bf16[1024,1024]{1,0:T(8,128)(2,1)}), bf16[1024,512]{1,0:T(8,128)(2,1)}) %reduce-scatter.17.cloned.1.call-update) | async-done | bytes 1048592 | tf_op jit(solution)/shard_map/reduce_scatter | solution.py:223
  465.7 4.3 all-gather.6
  471.3 5.7 reduce-scatter.21.cloned.1.call-done
  477.8 11.2 %reduce-scatter.19.cloned.1.call-done = bf16[32,8]{1,0:T(8,128)(2,1)} async-done(((bf16[64,8]{1,0:T(8,128)(2,1)}), bf16[32,8]{1,0:T(8,128)(2,1)}) %reduce-scatter.19.cloned.1.call-update) | async-done | bytes 528
  489.8 38.8 %all-reduce.22.cloned.1.call-done = (bf16[1,272,1024]{2,1,0:T(8,128)(2,1)}, bf16[1,272,1024]{2,1,0:T(8,128)(2,1)}) async-done(((bf16[1,272,1024]{2,1,0:T(8,128)(2,1)}, bf16[1,272,1024]{2,1,0:T(8,128)(2,1)}), (bf16[1,272,1024]{2,1,0:T(8,128)(2,1)}, bf16[1,272,1024]{2,1,0:T(8,128)(2,1)})) %all-reduce.22.cloned.1.call-update) | async-done | bytes 1114128 | tf_op jit(solution)/shard_map/psum | solution.py:122
  528.7 1.2 reduce_sum.210
  529.9 1.5 fusion.31
  532.1 1.6 fusion.65
  533.7 8.1 %all-reduce.11 = (bf16[1024]{0:T(1024)(128)(2,1)S(1)}, bf16[1024]{0:T(1024)(128)(2,1)S(1)}, bf16[1024]{0:T(1024)(128)(2,1)S(1)}, bf16[1024]{0:T(1024)(128)(2,1)S...) all-reduce(bf16[1024]{0:T(1024)(128)(2,1)S(1)} %get-tuple-element.4, ...), channel_id=7, replica_groups=mesh['fsdp'=2,'context'=4,'tensor'=4] {'fsdp'}, use_global_device_ids=true, to_apply=%region_25.26.clone | all-reduce | flops 6144 | bytes 24576
  542.2 12.7 %all-reduce.9 = (bf16[2,4,32]{2,1,0:T(4,128)(2,1)S(1)}, bf16[512]{0:T(512)(128)(2,1)S(1)}, bf16[4,128]{1,0:T(4,128)(2,1)S(1)}, bf16[512]{0:T(512)(128)(2,1)S(1)}...) all-reduce(bf16[2,4,32]{2,1,0:T(4,128)(2,1)S(1)} %copy.60, ...), channel_id=1, replica_groups=mesh['fsdp'=2,'context'=4,'tensor'=4] {'context'}, use_global_device_ids=true, to_apply=%region_21.22 | all-reduce | flops 3840 | bytes 15360 | tf_op jit(solution)/shard_map/psum | solution.py:244
  559.6 2.0 add_convert_fusion
  561.6 93.0 %all-reduce.24.cloned.1.call-done = (bf16[512,3,256]{2,0,1:T(8,128)(2,1)}, bf16[256,512]{1,0:T(8,128)(2,1)}, bf16[512,1024]{1,0:T(8,128)(2,1)}, bf16[1024,512]{1,0:T(8,128)(2,1)}) async-done(((bf16[512,3,256]{2,0,1:T(8,128)(2,1)}, bf16[256,512]{1,0:T(8,128)(2,1)}, bf16[512,1024]{1,0:T(8,128)(2,1)}, bf16[1024,512]{1,0:T(8,128)(2,1)}), (bf16[512,3,256]{2,0,1:T(8,128)(2,1)}, bf16[256,512]{1,0:T(8,128)(2,1)}, ...) | async-done | bytes 3145744 | tf_op jit(solution)/shard_map/psum | solution.py:243
  654.7 2.5 convert_element_type.338
  658.0 1.6 convert_element_type.347
  659.6 1.6 convert_element_type.351
  (223 shorter events, 29.4 us)
Async XLA Ops:
  7.2 18.0 %copy-start.48 = (u32[32]{0:T(128)S(1)}, u32[32]{0:T(128)}, u32[]{:S(2)}) copy-start(u32[32]{0:T(128)} %constant.50) | copy-start | bytes 388
  7.2 32.0 %copy-start.43 = (s32[1,272]{1,0:T(1,128)S(1)}, s32[1,272]{1,0:T(1,128)}, u32[]{:S(2)}) copy-start(s32[1,272]{1,0:T(1,128)} %param.16) | copy-start | bytes 3268
  7.2 32.0 %copy-start.24 = (bf16[256,512]{1,0:T(8,128)(2,1)S(1)}, bf16[256,512]{1,0:T(8,128)(2,1)}, u32[]{:S(2)}) copy-start(bf16[256,512]{1,0:T(8,128)(2,1)} %param.20) | copy-start | bytes 786436
  7.2 39.1 %copy-start.1 = (bf16[1,272,1024]{2,1,0:T(8,128)(2,1)S(1)}, bf16[1,272,1024]{2,1,0:T(8,128)(2,1)}, u32[]{:S(2)}) copy-start(bf16[1,272,1024]{2,1,0:T(8,128)(2,1)} %param.15) | copy-start | bytes 1671172
  7.2 40.1 %all-gather.11.cloned.1.call-start = ((), (), s32[]{:S(2)}) async-start(), calls=%async_computation.6 | async-start | bytes 2359296 | tf_op jit(solution)/shard_map/all_gather | solution.py:62
  8.0 118.6 %all-reduce.18.cloned.1.call-start = ((), (), s32[]{:S(2)}) async-start(), calls=%async_computation.7 | async-start | bytes 2228224 | tf_op jit(solution)/shard_map/psum | solution.py:113
  19.9 27.4 %copy-start.45 = (f32[2,1,512]{2,1,0:T(1,128)}, f32[2,1,512]{2,1,0:T(1,128)S(1)}, u32[]{:S(2)}) copy-start(f32[2,1,512]{2,1,0:T(1,128)S(1)} %convert_element_type.362) | copy-start | bytes 12292
  25.2 59.9 %copy-start.33 = (f32[4,64]{1,0:T(4,128)}, f32[4,64]{1,0:T(4,128)S(1)}, u32[]{:S(2)}) copy-start(f32[4,64]{1,0:T(4,128)S(1)} %copy.52) | copy-start | bytes 3076
  46.3 43.6 %copy-start.6 = (bf16[256,1024]{1,0:T(8,128)(2,1)}, bf16[256,1024]{1,0:T(8,128)(2,1)S(1)}, u32[]{:S(2)}) copy-start(bf16[256,1024]{1,0:T(8,128)(2,1)S(1)} %all_gather.52) | copy-start | bytes 1572868
  46.8 2.6 copy-start.39
  46.8 2.6 copy-start.35
  50.9 16.7 %copy-start.23 = (bf16[1,272,1,256]{3,1,2,0:T(8,128)(2,1)S(1)}, bf16[1,272,1,256]{3,1,2,0:T(8,128)(2,1)}, u32[]{:S(2)}) copy-start(bf16[1,272,1,256]{3,1,2,0:T(8,128)(2,1)} %slice.69) | copy-start | bytes 417796
  67.6 19.7 %copy-start.11 = (bf16[1,1088,256]{1,2,0:T(8,128)(2,1)}, bf16[1,1088,256]{1,2,0:T(8,128)(2,1)S(1)}, u32[]{:S(2)}) copy-start(bf16[1,1088,256]{1,2,0:T(8,128)(2,1)S(1)} %copy.50) | copy-start | bytes 1671172
  83.7 2.7 copy-start.4
  85.0 1.3 copy-start.9
  86.4 2.2 copy-start
  89.9 1.4 copy-start.19
  91.3 1.4 copy-start.50
  91.3 5.8 copy-start.51
  91.3 10.0 %copy-start.52 = (bf16[512]{0:T(512)(128)(2,1)S(1)}, bf16[512]{0:T(512)(128)(2,1)}, u32[]{:S(2)}) copy-start(bf16[512]{0:T(512)(128)(2,1)} %param.29) | copy-start | bytes 3076
  91.3 14.4 %copy-start.53 = (bf16[512]{0:T(512)(128)(2,1)S(1)}, bf16[512]{0:T(512)(128)(2,1)}, u32[]{:S(2)}) copy-start(bf16[512]{0:T(512)(128)(2,1)} %param.28) | copy-start | bytes 3076
  91.4 70.3 %all-gather.13.cloned.1.call-start = ((), (), s32[]{:S(2)}) async-start(), calls=%async_computation.8 | async-start | bytes 3145728 | tf_op jit(solution)/shard_map/all_gather | solution.py:64
  92.1 104.2 %all-gather.15.cloned.1.call-start = ((), (), s32[]{:S(2)}) async-start(), calls=%async_computation.9 | async-start | bytes 3145728 | tf_op jit(solution)/shard_map/all_gather | solution.py:65
  92.7 146.9 %all-reduce.20.cloned.1.call-start = ((), (), s32[]{:S(2)}) async-start(), calls=%async_computation.10 | async-start | bytes 2228224 | tf_op jit(solution)/shard_map/psum | solution.py:134
  105.7 55.9 %copy-start.47 = (f32[2,1,512]{2,1,0:T(1,128)}, f32[2,1,512]{2,1,0:T(1,128)S(1)}, u32[]{:S(2)}) copy-start(f32[2,1,512]{2,1,0:T(1,128)S(1)} %convert_element_type.365) | copy-start | bytes 12292
  110.1 131.9 %copy-start.26 = (f32[2,1,512]{2,1,0:T(1,128)}, f32[2,1,512]{2,1,0:T(1,128)S(1)}, u32[]{:S(2)}) copy-start(f32[2,1,512]{2,1,0:T(1,128)S(1)} %convert_element_type.364) | copy-start | bytes 12292
  128.1 113.9 %copy-start.28 = (f32[272]{0:T(512)}, f32[272]{0:T(512)S(1)}, u32[]{:S(2)}) copy-start(f32[272]{0:T(512)S(1)} %broadcast_multiply_fusion) | copy-start | bytes 3268
  128.4 113.6 %copy-start.38 = (f32[272]{0:T(512)}, f32[272]{0:T(512)S(1)}, u32[]{:S(2)}) copy-start(f32[272]{0:T(512)S(1)} %fusion.59) | copy-start | bytes 3268
  161.6 34.6 %copy-start.2 = (bf16[1,272,1024]{2,1,0:T(8,128)(2,1)S(1)}, bf16[1,272,1024]{2,1,0:T(8,128)(2,1)}, u32[]{:S(2)}) copy-start(bf16[1,272,1024]{2,1,0:T(8,128)(2,1)} %param.17) | copy-start | bytes 1671172
  164.1 36.1 %copy-start.56 = (f32[272,1024]{1,0:T(8,128)}, f32[272,1024]{1,0:T(8,128)S(1)}, u32[]{:S(2)}) copy-start(f32[272,1024]{1,0:T(8,128)S(1)} %convolution_add_fusion) | copy-start | bytes 3342340
  196.3 4.7 copy-start.13
  202.8 178.1 %reduce-scatter.13.cloned.1.call-start = ((), (), s32[]{:S(2)}) async-start(), calls=%async_computation.12 | async-start | bytes 786432 | tf_op jit(solution)/shard_map/reduce_scatter | solution.py:211
  239.6 2.4 copy-start.8
  242.0 1.1 copy-start.7
  245.1 4.5 copy-start.12
  245.1 8.4 %slice-start = ((s8[5013504]{0:T(1024)(128)(4,1)}), s8[4194304]{0:T(1024)(128)(4,1)S(1)}, s32[]{:S(2)}) async-start(s8[5013504]{0:T(1024)(128)(4,1)} %bitcast.150), calls=%async_computation.19 | async-start | bytes 8388608
  249.7 3.9 slice-start.1
  253.6 1.2 copy-start.10
  253.6 1.2 copy-start.34
  254.8 1.8 copy-start.5
  256.6 1.6 copy-start.20
  256.6 1.6 copy-start.31
  271.2 84.0 %copy-start.36 = (f32[272]{0:T(512)S(1)}, f32[272]{0:T(512)}, u32[]{:S(2)}) copy-start(f32[272]{0:T(512)} %copy-done.35) | copy-start | bytes 3268
  271.2 84.0 %copy-start.46 = (f32[2,1,512]{2,1,0:T(1,128)S(1)}, f32[2,1,512]{2,1,0:T(1,128)}, u32[]{:S(2)}) copy-start(f32[2,1,512]{2,1,0:T(1,128)} %copy-done.45) | copy-start | bytes 12292
  354.0 41.5 %reduce-scatter.11.cloned.1.call-start = ((), (), s32[]{:S(2)}) async-start(), calls=%async_computation.11 | async-start | bytes 2359296 | tf_op jit(solution)/shard_map/reduce_scatter | solution.py:205
  359.0 71.3 %reduce-scatter.15.cloned.1.call-start = ((), (), s32[]{:S(2)}) async-start(), calls=%async_computation.13 | async-start | bytes 3145728 | tf_op jit(solution)/shard_map/reduce_scatter | solution.py:217
  363.5 101.5 %reduce-scatter.17.cloned.1.call-start = ((), (), s32[]{:S(2)}) async-start(), calls=%async_computation.14 | async-start | bytes 3145728 | tf_op jit(solution)/shard_map/reduce_scatter | solution.py:223
  367.8 109.2 %reduce-scatter.21.cloned.1.call-start = ((), (), s32[]{:S(2)}) async-start(), calls=%async_computation.16 | async-start | bytes 98304
  369.2 4.4 copy-start.44
  369.2 119.8 %reduce-scatter.19.cloned.1.call-start = ((), (), s32[]{:S(2)}) async-start(), calls=%async_computation.15 | async-start | bytes 24576
  369.3 3.7 copy-start.15
  376.5 152.2 %all-reduce.22.cloned.1.call-start = ((), (), s32[]{:S(2)}) async-start(), calls=%async_computation.17 | async-start | bytes 2228224 | tf_op jit(solution)/shard_map/psum | solution.py:122
  376.6 1.6 copy-start.16
  380.8 273.9 %all-reduce.24.cloned.1.call-start = ((), (), s32[]{:S(2)}) async-start(), calls=%async_computation.18 | async-start | bytes 6291456 | tf_op jit(solution)/shard_map/psum | solution.py:243
  465.0 5.0 copy-start.55
  465.0 66.3 %copy-start.40 = (f32[272]{0:T(512)S(1)}, f32[272]{0:T(512)}, u32[]{:S(2)}) copy-start(f32[272]{0:T(512)} %copy-done.39) | copy-start | bytes 3268
  465.1 66.3 %copy-start.37 = (f32[272]{0:T(512)S(1)}, f32[272]{0:T(512)}, u32[]{:S(2)}) copy-start(f32[272]{0:T(512)} %copy-done.35) | copy-start | bytes 3268
  529.9 1.5 copy-start.3
  529.9 2.2 copy-start.32
  532.1 1.6 copy-start.41
  532.1 1.6 copy-start.42
  654.7 2.5 copy-start.25
  654.7 3.4 copy-start.18
  658.0 1.6 copy-start.17
  (8 other events, 5.6 us)
Sparse Core Ops, SparseCore 0:
  9.6 31.2 all-gather.10
  91.4 35.1 all-reduce.17
  128.2 33.3 all-gather.12
  163.1 33.1 all-gather.14
  202.9 36.6 all-reduce.19
  354.1 12.3 reduce-scatter.12
  369.4 26.0 reduce-scatter.10
  398.3 31.8 reduce-scatter.14
  433.2 31.8 reduce-scatter.16
  467.1 9.8 reduce-scatter.20
  479.2 9.7 reduce-scatter.18
  491.8 36.8 all-reduce.21
  531.5 123.1 all-reduce.23
where the time goes:
time: 669 us; the launch traced here: 668 us
  waiting for transfers between devices  353 us (53%)
  blocking collectives  191 us (29%)
  matrix products  45.6 us (7%)
  other arithmetic  32.9 us (5%)
  local copies, waits for them, and re-layouts  27.9 us (4%)
  between operations  16.6 us (2%)
    unnamed x3, blocking collectives  103 us
    psum x1, waiting for transfers between devices, body(): lax.psum(shards[0].astype(jnp.bfloat16), 'context').astype(jnp.float32)  93 us
    psum x1, waiting for transfers between devices, body(): lax.psum(mlp_part.astype(jnp.bfloat16), 'tensor').astype(jnp.float32)  38.8 us
    psum x1, waiting for transfers between devices, body(): grad_normed2 = lax.psum(grad_normed2, 'tensor')  35.9 us
    reduce_scatter x1, waiting for transfers between devices, body(): lax.psum_scatter(grad_w_proj.astype(jnp.bfloat16), 'fsdp', scatter_dimens...  34.8 us
    reduce_scatter x1, waiting for transfers between devices, body(): lax.psum_scatter(grad_w_fc.astype(jnp.bfloat16), 'fsdp', scatter_dimensio...  34.8 us
    all_gather x1, waiting for transfers between devices, body(): lax.all_gather(w_fc, 'fsdp', axis=0, tiled=True)  33.3 us
    all_gather x1, waiting for transfers between devices, body(): lax.all_gather(w_proj, 'fsdp', axis=1, tiled=True)  32.2 us
  transfers between devices with their start and end apart: 13, of which 11 were waited for; matrix products, arithmetic and copies ran while one was open for 7% of the time, Pallas kernels for 0%

commit v1 on v0

--- a/solution.py
+++ b/solution.py
@@ -271,9 +271,237 @@
     )
 
 
+def swap(values, axis, distance):
+    size = lax.axis_size(axis)
+    return lax.ppermute(values, axis, [(i, i ^ distance) for i in range(size)])
+
+
+def after(values, earlier):
+    return lax.optimization_barrier((values, earlier))[0]
+
+
+def sum_four(part):
+    half = part.shape[-1] // 2
+    low = lax.axis_index("tensor") % 2 == 0
+    left, right = part[:, :half], part[:, half:]
+    keep = jnp.where(low, left, right)
+    got = swap(jnp.where(low, right, left), "tensor", 1)
+    pair = (keep.astype(jnp.float32) + got.astype(jnp.float32)).astype(jnp.bfloat16)
+    far = swap(pair, "tensor", 2)
+    mine = (pair.astype(jnp.float32) + far.astype(jnp.float32)).astype(jnp.bfloat16)
+    other = swap(mine, "tensor", 1)
+    return jnp.concatenate(
+        (jnp.where(low, mine, other), jnp.where(low, other, mine)), axis=-1
+    ).astype(jnp.float32)
+
+
+def dot_to(left, right, dims):
+    return lax.dot_general(left, right, (dims, ((), ())), preferred_element_type=jnp.float32)
+
+
+def norm_parts(values):
+    mean = jnp.mean(values, axis=-1, keepdims=True)
+    centred = values - mean
+    spread = jnp.mean(centred * centred, axis=-1, keepdims=True)
+    rate = lax.rsqrt(spread + EPSILON)
+    return centred * rate, rate
+
+
+def norm_back(grad, nhat, rate, gain):
+    scaled = grad * gain
+    inner = (
+        scaled
+        - jnp.mean(scaled, axis=-1, keepdims=True)
+        - nhat * jnp.mean(scaled * nhat, axis=-1, keepdims=True)
+    )
+    return rate * inner, jnp.sum(grad * nhat, axis=0), jnp.sum(grad, axis=0)
+
+
+def fast_body(
+    tokens,
+    segments,
+    cotangent,
+    w_qkv,
+    b_qv,
+    w_out,
+    b_out,
+    w_fc,
+    b_fc,
+    w_proj,
+    b_proj,
+    ln1_gain,
+    ln1_shift,
+    ln2_gain,
+    ln2_shift,
+):
+    f32, bf16 = jnp.float32, jnp.bfloat16
+    rows, width = tokens.shape[1:]
+    half = width // 2
+    heads = b_qv.shape[1]
+    local = heads * HD
+    first = lax.axis_index("fsdp") == 0
+
+    def turn(values):
+        other = jnp.concatenate((values[:, half:], values[:, :half]), axis=1)
+        return jnp.where(first, values, other)
+
+    def in_order(mine, theirs, axis):
+        return jnp.where(
+            first,
+            jnp.concatenate((mine, theirs), axis=axis),
+            jnp.concatenate((theirs, mine), axis=axis),
+        )
+
+    vectors = (ln1_gain, ln1_shift, ln2_gain, ln2_shift, b_out, b_proj)
+    packed = jnp.concatenate(vectors + (b_qv.reshape(-1), b_fc.reshape(-1)))
+    packed_far = swap(packed, "fsdp", 1)
+    flat_qkv = w_qkv.reshape(half, 3 * local)
+    qkv_far = swap(flat_qkv, "fsdp", 1)
+    out_far = swap(after(w_out, qkv_far), "fsdp", 1)
+    fc_far = swap(after(w_fc, out_far), "fsdp", 1)
+    proj_far = swap(after(w_proj, fc_far), "fsdp", 1)
+
+    def whole(index):
+        far = packed_far[index * half : (index + 1) * half]
+        return jnp.concatenate((vectors[index], far)).astype(f32)
+
+    gain_one, shift_one, gain_two, shift_two, bias_out, bias_proj = [whole(i) for i in range(6)]
+    at = 6 * half
+    bias_qv = in_order(b_qv, packed_far[at : at + b_qv.size].reshape(b_qv.shape), 2)
+    bias_qv = bias_qv.astype(f32).reshape(2, local)
+    at += b_qv.size
+    bias_fc = in_order(b_fc, packed_far[at:].reshape(b_fc.shape), 1).astype(f32).reshape(-1)
+
+    base = turn(tokens[0]).astype(f32)
+    cot = turn(cotangent[0])
+    nhat_one, rate_one = norm_parts(base)
+    normed1 = (nhat_one * gain_one + shift_one).astype(bf16)
+    qkv_all = jnp.concatenate((flat_qkv, qkv_far), axis=0)
+    bias_row = jnp.concatenate((bias_qv[0], jnp.zeros((local,), f32), bias_qv[1]))
+    projected = (dot_to(normed1, qkv_all, ((1,), (0,))) + bias_row).astype(bf16)
+
+    send = jnp.transpose(projected.reshape(rows, 3, heads, HD), (2, 0, 1, 3))
+    send = send.reshape(heads, rows, 3 * HD)
+    seg_cols = jnp.broadcast_to(segments[0].astype(bf16)[None, :, None], (heads, rows, HD))
+    send = jnp.concatenate((send, seg_cols), axis=2)
+    got = lax.all_to_all(send, "context", 0, 0, tiled=True).reshape(heads * rows, 4 * HD)
+    queries, keys, values = got[:, :HD], got[:, HD : 2 * HD], got[:, 2 * HD : 3 * HD]
+    seg_all = got[:, 3 * HD]
+    position = jnp.arange(heads * rows, dtype=jnp.int32)
+    seen = (seg_all[:, None] == seg_all[None, :]) & (position[None, :] <= position[:, None])
+    scores = jnp.where(
+        seen, SCORE_SCALE * dot_to(queries, keys, ((1,), (1,))), -MASK_FILL
+    )
+    row_top = jnp.max(scores, axis=-1, keepdims=True)
+    exponent = jnp.exp(scores - row_top)
+    row_total = jnp.sum(exponent, axis=-1, keepdims=True)
+    pfull = exponent / row_total
+    probs = pfull.astype(bf16)
+    att_head = dot_to(probs, values, ((1,), (0,))).astype(bf16)
+    att = lax.all_to_all(att_head.reshape(heads, rows, HD), "context", 0, 0, tiled=True)
+    attended = jnp.transpose(att, (1, 0, 2)).reshape(rows, local)
+
+    out_all = jnp.concatenate((w_out, out_far), axis=1)
+    attn_part = dot_to(attended, out_all, ((1,), (0,))).astype(bf16)
+    hidden = base + sum_four(attn_part) + bias_out
+    nhat_two, rate_two = norm_parts(hidden)
+    normed2 = (nhat_two * gain_two + shift_two).astype(bf16)
+    fc_all = jnp.concatenate((w_fc, fc_far), axis=0)
+    proj_all = jnp.concatenate((w_proj, proj_far), axis=1)
+    pre_act = dot_to(normed2, fc_all, ((1,), (0,))) + bias_fc
+    activ, gelu_pull = jax.vjp(gelu_tanh, pre_act)
+    activ = activ.astype(bf16)
+    grad_activ = dot_to(cot, proj_all, ((1,), (1,)))
+    grad_pre = gelu_pull(grad_activ)[0].astype(bf16)
+    grad_n2 = sum_four(dot_to(grad_pre, fc_all, ((1,), (1,))).astype(bf16))
+    mlp_part = dot_to(activ, proj_all, ((1,), (0,))).astype(bf16)
+    mixed = turn((hidden + sum_four(mlp_part) + bias_proj).astype(bf16))
+
+    def reduced(mine, theirs, earlier):
+        total = mine + swap(theirs.astype(bf16), "fsdp", 1).astype(f32)
+        total = total.astype(bf16)
+        if earlier is not None:
+            total = after(total, earlier)
+        return lax.psum(total, "context")
+
+    grad_proj = dot_to(activ, cot, ((0,), (0,)))
+    proj_sum = reduced(grad_proj[:, :half], grad_proj[:, half:], None)
+    grad_fc = dot_to(normed2, grad_pre, ((0,), (0,)))
+    fc_sum = reduced(grad_fc[:half], grad_fc[half:], proj_sum)
+
+    grad_out = cot.astype(f32)
+    back_two, grad_gain_two, grad_shift_two = norm_back(grad_n2, nhat_two, rate_two, gain_two)
+    grad_hidden = grad_out + back_two
+    grad_branch = grad_hidden.astype(bf16)
+    grad_att = dot_to(grad_branch, out_all, ((1,), (1,))).astype(bf16)
+    grad_att = jnp.transpose(grad_att.reshape(rows, heads, HD), (1, 0, 2))
+    grad_head = lax.all_to_all(grad_att, "context", 0, 0, tiled=True).reshape(heads * rows, HD)
+    grad_w_out = dot_to(attended, grad_branch, ((0,), (0,)))
+    out_sum = reduced(grad_w_out[:, :half], grad_w_out[:, half:], fc_sum)
+
+    grad_probs = dot_to(grad_head, values, ((1,), (1,)))
+    row_delta = jnp.sum(grad_probs * pfull, axis=-1, keepdims=True)
+    grad_scores = (pfull * (grad_probs - row_delta)).astype(bf16)
+    grad_q = SCORE_SCALE * dot_to(grad_scores, keys, ((1,), (0,)))
+    grad_k = SCORE_SCALE * dot_to(grad_scores, queries, ((0,), (0,)))
+    grad_v = dot_to(probs, grad_head, ((0,), (0,)))
+    back = jnp.concatenate((grad_q, grad_k, grad_v), axis=1).astype(bf16)
+    back = lax.all_to_all(back.reshape(heads, rows, 3 * HD), "context", 0, 0, tiled=True)
+    back = jnp.transpose(back.reshape(heads, rows, 3, HD), (1, 2, 0, 3)).reshape(rows, 3 * local)
+    grad_n1 = sum_four(dot_to(back, qkv_all, ((1,), (1,))).astype(bf16))
+    grad_qkv = dot_to(normed1, back, ((0,), (0,)))
+    qkv_sum = reduced(grad_qkv[:half], grad_qkv[half:], out_sum)
+    back_one, grad_gain_one, grad_shift_one = norm_back(grad_n1, nhat_one, rate_one, gain_one)
+    grad_tokens = turn(grad_hidden + back_one)
+
+    grad_b_qkv = jnp.sum(back.astype(f32), axis=0).reshape(3, heads, HD)
+    grad_b_qv = jnp.stack((grad_b_qkv[0], grad_b_qkv[2]))
+    grad_b_fc = jnp.sum(grad_pre.astype(f32), axis=0).reshape(b_fc.shape[0], -1)
+    sums = (
+        jnp.sum(grad_out, axis=0),
+        jnp.sum(grad_hidden, axis=0),
+        grad_gain_one,
+        grad_shift_one,
+        grad_gain_two,
+        grad_shift_two,
+    )
+
+    def split(values, axis):
+        left, right = jnp.split(values, 2, axis=axis)
+        return jnp.where(first, left, right), jnp.where(first, right, left)
+
+    qv_mine, qv_far = split(grad_b_qv, 2)
+    fc_mine, fc_theirs = split(grad_b_fc, 1)
+    near = jnp.concatenate([v[:half] for v in sums] + [qv_mine.reshape(-1), fc_mine.reshape(-1)])
+    away = jnp.concatenate([v[half:] for v in sums] + [qv_far.reshape(-1), fc_theirs.reshape(-1)])
+    small = near + swap(away, "fsdp", 1)
+    small = small + swap(small, "context", 1)
+    small = small + swap(small, "context", 2)
+    pieces = [small[i * half : (i + 1) * half] for i in range(6)]
+    at = 6 * half
+    return (
+        mixed[None],
+        grad_tokens[None],
+        qkv_sum.astype(f32).reshape(half, 3, local),
+        small[at : at + b_qv.size].reshape(b_qv.shape),
+        out_sum.astype(f32),
+        pieces[1],
+        fc_sum.astype(f32),
+        small[at + b_qv.size :].reshape(b_fc.shape),
+        proj_sum.astype(f32),
+        pieces[0],
+        pieces[2],
+        pieces[3],
+        pieces[4],
+        pieces[5],
+    )
+
+
 def solution(mesh):
+    sizes = mesh.shape
+    even = sizes["fsdp"] == 2 and sizes["tensor"] == 4 and sizes["context"] == 4
     return jax.shard_map(
-        body,
+        fast_body if even else body,
         mesh=mesh,
         in_specs=(
             P("fsdp", "context", None),

time: 669 us -> 419 us (0.63)
  blocking collectives: 191 us -> 0 us
  waiting for transfers between devices: 353 us -> 236 us
  starting transfers between devices: 0.93 us -> 36.2 us
  local copies, waits for them, and re-layouts: 27.9 us -> 61.5 us
  matrix products: 45.6 us -> 28.3 us
  other arithmetic: 32.9 us -> 40.3 us
    unnamed x3 -> x0, blocking collectives: 103 us -> none
    ppermute x0 -> x24, waiting for transfers between devices: none -> 100 us  [swap(): return lax.ppermute(values, axis, [(i, i ^ distance) for i in range(size)])]
    reduce_scatter x4 -> x0, waiting for transfers between devices: 84.2 us -> none  [the longest x1 34.8 us: body(): lax.psum_scatter(grad_w_proj.astype(jnp.bfloat16), 'fsdp', scatter_dimens...]
    all_gather x11 -> x0, blocking collectives: 74.8 us -> none  [the longest x1 16.4 us: body(): lax.all_gather(values_low, 'context', axis=1, tiled=True)]
    psum x4, waiting for transfers between devices: 184 us -> 110 us  [reduced(): return lax.psum(total, 'context')]
    all_gather x3 -> x0, waiting for transfers between devices: 65.4 us -> none  [the longest x1 33.3 us: body(): lax.all_gather(w_fc, 'fsdp', axis=0, tiled=True)]
    all_to_all x0 -> x4, waiting for transfers between devices: none -> 26.4 us  [the longest x1 13.5 us: fast_body(): lax.all_to_all(send, 'context', 0, 0, tiled=True)]
    ppermute x0 -> x24, starting transfers between devices: none -> 20.3 us  [swap(): return lax.ppermute(values, axis, [(i, i ^ distance) for i in range(size)])]
  transfers between devices with their start and end apart: 13 -> 32, of which waited for: 11 -> 22; matrix products, arithmetic and copies ran while one was open for 7% -> 22% of each run, Pallas kernels for 0% -> 0%
where the time goes in v1:
time: 419 us; the launch traced here: 418 us
  waiting for transfers between devices  236 us (56%)
  local copies, waits for them, and re-layouts  61.5 us (15%)
  other arithmetic  40.3 us (10%)
  starting transfers between devices  36.2 us (9%)
  matrix products  28.3 us (7%)
  between operations  14.9 us (4%)
    psum x4, waiting for transfers between devices, reduced(): return lax.psum(total, 'context')  110 us
    ppermute x24, waiting for transfers between devices, swap(): return lax.ppermute(values, axis, [(i, i ^ distance) for i in range(size)])  100 us
    unnamed x165, local copies, waits for them, and re-layouts  34.3 us
    dot_general x18, matrix products, dot_to(): lax.dot_general(left, right, (dims, ((), ())), preferred_element_type=jnp...  28.3 us
    ppermute x24, starting transfers between devices, swap(): return lax.ppermute(values, axis, [(i, i ^ distance) for i in range(size)])  20.3 us
    all_to_all x1, waiting for transfers between devices, fast_body(): lax.all_to_all(send, 'context', 0, 0, tiled=True)  13.5 us
  transfers between devices with their start and end apart: 32, of which 22 were waited for; matrix products, arithmetic and copies ran while one was open for 22% of the time, Pallas kernels for 0%

profile of v1, /device:TPU:0, one launch (start us, length us, event | category | flops | bytes accessed | tf_op | source)
XLA Modules:
  0.0 417.5 jit_solution(8565138531932072020)
XLA Ops:
  14.2 3.0 collective-permute-start
  17.2 1.4 copy.115
  21.4 16.3 %collective-permute-done.1 = bf16[512,768]{0,1:T(8,128)(2,1)S(1)} collective-permute-done((bf16[512,768]{0,1:T(8,128)(2,1)S(1)}, bf16[512,768]{0,1:T(8,128)(2,1)S(1)}, u32[]{:S(2)}, u32[]{:S(2)}) %collective-permute-start.1) | collective-permute-done | bytes 786464 | tf_op jit(solution)/shard_map/ppermute | solution.py:276
  40.2 4.9 %all-to-all-start = ((bf16[4,272,256]{2,1,0:T(8,128)(2,1)}), bf16[4,272,256]{2,1,0:T(8,128)(2,1)S(1)}, u32[]{:S(2)}, u32[]{:S(2)}) async-start(bf16[4,272,256]{2,1,0:T(8,128)(2,1)} %copy.118), calls=%async_computation | async-start | bytes 1114112 | tf_op jit(solution)/shard_map/all_to_all | solution.py:387
  45.6 13.5 %all-to-all-done = bf16[4,272,256]{2,1,0:T(8,128)(2,1)S(1)} async-done(((bf16[4,272,256]{2,1,0:T(8,128)(2,1)}), bf16[4,272,256]{2,1,0:T(8,128)(2,1)S(1)}, u32[]{:S(2)}, u32[]{:S(2)}) %all-to-all-start) | async-done | bytes 557088 | tf_op jit(solution)/shard_map/all_to_all | solution.py:387
  59.1 3.1 convolution_multiply_fusion
  62.5 6.7 %copy.119 = f32[1088,1088]{1,0:T(8,128)} copy(f32[1088,1088]{0,1:T(8,128)} %convolution_multiply_fusion) | data formatting | bytes 9469952 | tf_op jit(solution)/shard_map/mul | solution.py:393
  69.2 3.4 fusion.9
  74.2 1.3 copy-done.2
  75.5 4.6 %fusion.3 = (bf16[1088,1088]{1,0:T(8,128)(2,1)}, f32[1088,1088]{1,0:T(8,128)S(1)}) fusion(f32[1088,1088]{0,1:T(8,128)S(1)} %copy-done.2, f32[1088]{0:T(1024)S(1)} %fusion.8, f32[1088]{0:T(1024)S(1)} %fusion.9, bf16[1088]{0:T(1024)(128)(2,1)S(1)} %slice_reduce_fusion, f32[1088,1088]{1,0:T(8,128)S(1)} %copy-done), kind=kLoop, calls=%fused_computation.10 | loop fusion | flops 17756160 | bytes 16583296 | tf_op jit(solution)/shard_map/convert_element_type | solution.py:399
  80.1 2.3 copy-done.1
  84.1 3.5 all-to-all-start.1
  87.7 6.4 %all-to-all-done.1 = bf16[4,272,64]{1,2,0:T(8,128)(2,1)S(1)} async-done(((bf16[4,272,64]{1,2,0:T(8,128)(2,1)}), bf16[4,272,64]{1,2,0:T(8,128)(2,1)S(1)}, u32[]{:S(2)}, u32[]{:S(2)}) %all-to-all-start.1) | async-done | bytes 139296 | tf_op jit(solution)/shard_map/all_to_all | solution.py:401
  97.4 1.6 collective-permute-start.4
  99.7 6.5 %collective-permute-done.4 = bf16[272,512]{1,0:T(8,128)(2,1)S(1)} collective-permute-done((bf16[272,512]{1,0:T(8,128)(2,1)S(1)}, bf16[272,512]{1,0:T(8,128)(2,1)S(1)}, u32[]{:S(2)}, u32[]{:S(2)}) %collective-permute-start.4) | collective-permute-done | bytes 278560 | tf_op jit(solution)/shard_map/ppermute | solution.py:276
  106.4 15.9 %collective-permute-done.6 = bf16[512,1024]{1,0:T(8,128)(2,1)S(1)} collective-permute-done((bf16[512,1024]{1,0:T(8,128)(2,1)S(1)}, bf16[512,1024]{1,0:T(8,128)(2,1)S(1)}, u32[]{:S(2)}, u32[]{:S(2)}) %collective-permute-start.6) | collective-permute-done | bytes 1048608 | tf_op jit(solution)/shard_map/ppermute | solution.py:276
  124.5 22.6 %collective-permute-done.7 = bf16[1024,512]{1,0:T(8,128)(2,1)S(1)} collective-permute-done((bf16[1024,512]{1,0:T(8,128)(2,1)S(1)}, bf16[1024,512]{1,0:T(8,128)(2,1)S(1)}, u32[]{:S(2)}, u32[]{:S(2)}) %collective-permute-start.7) | collective-permute-done | bytes 1048608 | tf_op jit(solution)/shard_map/ppermute | solution.py:276
  147.2 2.2 convert_reduce_fusion.5
  152.0 1.6 collective-permute-start.12
  155.3 6.3 %collective-permute-done.12 = bf16[272,512]{1,0:T(8,128)(2,1)} collective-permute-done((bf16[272,512]{1,0:T(8,128)(2,1)S(1)}, bf16[272,512]{1,0:T(8,128)(2,1)}, u32[]{:S(2)}, u32[]{:S(2)}) %collective-permute-start.12) | collective-permute-done | bytes 278560 | tf_op jit(solution)/shard_map/ppermute | solution.py:276
  162.8 4.1 collective-permute-done.9
  168.1 1.4 collective-permute-done.10
  169.6 2.1 fusion.59
  175.1 3.6 all-to-all-start.2
  178.7 2.7 fusion.90
  181.4 2.0 copy-done.4
  185.1 1.4 all-to-all-done.2
  188.2 1.9 reshape.691
  190.1 3.6 multiply_reduce_fusion
  194.3 1.4 copy-done.3
  197.2 2.6 fusion.12
  200.2 2.8 convolution_convert_fusion.4
  204.1 3.5 all-to-all-start.3
  207.7 2.6 fusion.93
  210.3 2.0 copy-done.23
  213.4 1.4 collective-permute-start.19
  214.8 2.6 fusion.17
  217.4 5.0 %all-to-all-done.3 = bf16[4,272,192]{2,1,0:T(8,128)(2,1)S(1)} async-done(((bf16[4,272,192]{2,1,0:T(8,128)(2,1)}), bf16[4,272,192]{2,1,0:T(8,128)(2,1)S(1)}, u32[]{:S(2)}, u32[]{:S(2)}) %all-to-all-start.3) | async-done | bytes 417824 | tf_op jit(solution)/shard_map/all_to_all | solution.py:449
  222.9 1.3 copy-done.36
  224.2 1.8 convolution_convert_fusion.3
  226.7 1.3 constant_dynamic-update-slice_fusion.7
  228.6 1.3 constant_dynamic-update-slice_fusion.9
  229.9 1.8 add_convert_fusion.4
  231.7 1.5 collective-permute-start.15
  233.2 4.7 %collective-permute-done.19 = bf16[512,1024]{1,0:T(8,128)(2,1)} collective-permute-done((bf16[512,1024]{1,0:T(8,128)(2,1)}, bf16[512,1024]{1,0:T(8,128)(2,1)}, u32[]{:S(2)}, u32[]{:S(2)}) %collective-permute-start.19) | collective-permute-done | bytes 1048608 | tf_op jit(solution)/shard_map/ppermute | solution.py:276
  237.9 3.2 fusion.18
  241.1 28.7 %all-reduce.5.cloned.1.call-done = bf16[1024,512]{1,0:T(8,128)(2,1)} async-done(((bf16[1024,512]{1,0:T(8,128)(2,1)}), bf16[1024,512]{1,0:T(8,128)(2,1)}) %all-reduce.5.cloned.1.call-update) | async-done | bytes 1048592 | tf_op jit(solution)/shard_map/psum | solution.py:425
  276.1 2.2 fusion.45
  279.5 1.5 collective-permute-start.17
  282.6 1.3 constant_dynamic-update-slice_fusion.21
  289.0 16.1 %collective-permute-done.18 = bf16[256,512]{1,0:T(8,128)(2,1)S(1)} collective-permute-done((bf16[256,512]{1,0:T(8,128)(2,1)S(1)}, bf16[256,512]{1,0:T(8,128)(2,1)S(1)}, u32[]{:S(2)}, u32[]{:S(2)}) %collective-permute-start.18) | collective-permute-done | bytes 262176 | tf_op jit(solution)/shard_map/ppermute | solution.py:276
  305.9 18.3 %all-reduce.7.cloned.1.call-done = bf16[512,1024]{1,0:T(8,128)(2,1)} async-done(((bf16[512,1024]{1,0:T(8,128)(2,1)}), bf16[512,1024]{1,0:T(8,128)(2,1)}) %all-reduce.7.cloned.1.call-update) | async-done | bytes 1048592 | tf_op jit(solution)/shard_map/psum | solution.py:425
  324.2 1.6 fusion.19
  325.8 36.0 %all-reduce.9.cloned.1.call-done = bf16[256,512]{1,0:T(8,128)(2,1)} async-done(((bf16[256,512]{1,0:T(8,128)(2,1)}), bf16[256,512]{1,0:T(8,128)(2,1)}) %all-reduce.9.cloned.1.call-update) | async-done | bytes 262160 | tf_op jit(solution)/shard_map/psum | solution.py:425
  363.0 1.3 constant_dynamic-update-slice_fusion.11
  364.3 1.5 collective-permute-start.21
  365.8 2.5 collective-permute-done.21
  368.3 1.4 collective-permute-start.22
  369.8 1.6 convert_element_type.392
  372.4 1.7 collective-permute-start.23
  375.3 2.7 collective-permute-done.23
  379.3 1.6 convert_element_type.391
  381.7 26.7 %all-reduce.11.cloned.1.call-done = bf16[512,3,256]{0,2,1:T(8,128)(2,1)} async-done(((bf16[512,3,256]{0,2,1:T(8,128)(2,1)}), bf16[512,3,256]{0,2,1:T(8,128)(2,1)}) %all-reduce.11.cloned.1.call-update) | async-done | bytes 786448 | tf_op jit(solution)/shard_map/psum | solution.py:425
  408.4 2.5 copy.133
  (302 shorter events, 63.1 us)
Async XLA Ops:
  7.2 11.5 %copy-start.10 = (bf16[1,272,1024]{2,1,0:T(8,128)(2,1)S(1)}, bf16[1,272,1024]{2,1,0:T(8,128)(2,1)}, u32[]{:S(2)}) copy-start(bf16[1,272,1024]{2,1,0:T(8,128)(2,1)} %param.15) | copy-start | bytes 1671172
  14.2 6.2 %collective-permute-start = (bf16[3840]{0:T(1024)(128)(2,1)S(1)}, bf16[3840]{0:T(1024)(128)(2,1)S(1)}, u32[]{:S(2)}, u32[]{:S(2)}) collective-permute-start(bf16[3840]{0:T(1024)(128)(2,1)S(1)} %dynamic-update-slice.29), channel_id=1, source_target_pairs={{0,16},{16,0},{1,17},{17,1},{2,18},{18,2},{3,19},{19,3},{4,20},{20... | collective-permute-start | bytes 23048 | tf_op jit(solution)/shard_map/ppermute | solution.py:276
  18.6 19.1 %copy-start.35 = (bf16[512,3,256]{0,2,1:T(8,128)(2,1)}, bf16[512,3,256]{0,2,1:T(8,128)(2,1)S(1)}, u32[]{:S(2)}) copy-start(bf16[512,3,256]{0,2,1:T(8,128)(2,1)S(1)} %copy.115) | copy-start | bytes 2359300
  18.6 19.1 %collective-permute-start.1 = (bf16[512,768]{0,1:T(8,128)(2,1)S(1)}, bf16[512,768]{0,1:T(8,128)(2,1)S(1)}, u32[]{:S(2)}, u32[]{:S(2)}) collective-permute-start(bf16[512,768]{0,1:T(8,128)(2,1)S(1)} %bitcast.135), channel_id=1, source_target_pairs={{0,16},{16,0},{1,17},{17,1},{2,18},{18,2},{3,19},{19,3},{4,20},{20... | collective-permute-start | bytes 2359304 | tf_op jit(solution)/shard_map/ppermute | solution.py:276
  21.4 17.0 %copy-start.44 = (f32[1024]{0:T(1024)}, f32[1024]{0:T(1024)S(1)}, u32[]{:S(2)}) copy-start(f32[1024]{0:T(1024)S(1)} %get-tuple-element.189) | copy-start | bytes 12292
  39.1 6.0 %copy-start.39 = (bf16[256,512]{1,0:T(8,128)(2,1)S(1)}, bf16[256,512]{1,0:T(8,128)(2,1)}, u32[]{:S(2)}) copy-start(bf16[256,512]{1,0:T(8,128)(2,1)} %param.20) | copy-start | bytes 786436
  40.2 18.9 %all-to-all-start = ((bf16[4,272,256]{2,1,0:T(8,128)(2,1)}), bf16[4,272,256]{2,1,0:T(8,128)(2,1)S(1)}, u32[]{:S(2)}, u32[]{:S(2)}) async-start(bf16[4,272,256]{2,1,0:T(8,128)(2,1)} %copy.118), calls=%async_computation | async-start | bytes 1114112 | tf_op jit(solution)/shard_map/all_to_all | solution.py:387
  45.1 42.6 %collective-permute-start.2 = (bf16[256,512]{1,0:T(8,128)(2,1)S(1)}, bf16[256,512]{1,0:T(8,128)(2,1)S(1)}, u32[]{:S(2)}, u32[]{:S(2)}) collective-permute-start(bf16[256,512]{1,0:T(8,128)(2,1)S(1)} %copy-done.39), channel_id=1, source_target_pairs={{0,16},{16,0},{1,17},{17,1},{2,18},{18,2},{3,19},{19,3},{4,20},{20... | collective-permute-start | bytes 786440 | tf_op jit(solution)/shard_map/ppermute | solution.py:276
  69.2 3.9 copy-start
  84.1 10.0 %all-to-all-start.1 = ((bf16[4,272,64]{1,2,0:T(8,128)(2,1)}), bf16[4,272,64]{1,2,0:T(8,128)(2,1)S(1)}, u32[]{:S(2)}, u32[]{:S(2)}) async-start(bf16[4,272,64]{1,2,0:T(8,128)(2,1)} %copy.120), calls=%async_computation.1 | async-start | bytes 393216 | tf_op jit(solution)/shard_map/all_to_all | solution.py:401
  87.7 7.8 %copy-start.15 = (bf16[256,1024]{1,0:T(8,128)(2,1)}, bf16[256,1024]{1,0:T(8,128)(2,1)S(1)}, u32[]{:S(2)}) copy-start(bf16[256,1024]{1,0:T(8,128)(2,1)S(1)} %constant_dynamic-update-slice_fusion) | copy-start | bytes 1572868
  87.7 6.9 %copy-start.9 = (bf16[1,272,1024]{2,1,0:T(8,128)(2,1)S(1)}, bf16[1,272,1024]{2,1,0:T(8,128)(2,1)}, u32[]{:S(2)}) copy-start(bf16[1,272,1024]{2,1,0:T(8,128)(2,1)} %param.17) | copy-start | bytes 1671172
  94.5 2.7 collective-permute-start.3
  96.7 25.6 %collective-permute-start.6 = (bf16[512,1024]{1,0:T(8,128)(2,1)S(1)}, bf16[512,1024]{1,0:T(8,128)(2,1)S(1)}, u32[]{:S(2)}, u32[]{:S(2)}) collective-permute-start(bf16[512,1024]{1,0:T(8,128)(2,1)S(1)} %copy-done.32), channel_id=1, source_target_pairs={{0,16},{16,0},{1,17},{17,1},{2,18},{18,2},{3,19},{19,3},{4,20},{20... | collective-permute-start | bytes 3145736 | tf_op jit(solution)/shard_map/ppermute | solution.py:276
  97.4 8.8 %collective-permute-start.4 = (bf16[272,512]{1,0:T(8,128)(2,1)S(1)}, bf16[272,512]{1,0:T(8,128)(2,1)S(1)}, u32[]{:S(2)}, u32[]{:S(2)}) collective-permute-start(bf16[272,512]{1,0:T(8,128)(2,1)S(1)} %add_convert_fusion.10), channel_id=1, source_target_pairs={{0,2},{1,3},{2,0},{3,1},{4,6},{5,7},{6,4},{7,5},{8,10},{9,11},{10,... | collective-permute-start | bytes 835592 | tf_op jit(solution)/shard_map/ppermute | solution.py:276
  99.0 7.3 %copy-start.65 = (bf16[4,128]{1,0:T(4,128)(2,1)S(1)}, bf16[4,128]{1,0:T(4,128)(2,1)}, u32[]{:S(2)}) copy-start(bf16[4,128]{1,0:T(4,128)(2,1)} %param.23) | copy-start | bytes 3076
  99.0 7.3 %copy-start.62 = (bf16[512]{0:T(512)(128)(2,1)S(1)}, bf16[512]{0:T(512)(128)(2,1)}, u32[]{:S(2)}) copy-start(bf16[512]{0:T(512)(128)(2,1)} %param.28) | copy-start | bytes 3076
  99.1 7.3 %copy-start.63 = (bf16[512]{0:T(512)(128)(2,1)S(1)}, bf16[512]{0:T(512)(128)(2,1)}, u32[]{:S(2)}) copy-start(bf16[512]{0:T(512)(128)(2,1)} %param.29) | copy-start | bytes 3076
  106.3 16.6 %collective-permute-start.5 = (bf16[272,512]{1,0:T(8,128)(2,1)S(1)}, bf16[272,512]{1,0:T(8,128)(2,1)S(1)}, u32[]{:S(2)}, u32[]{:S(2)}) collective-permute-start(bf16[272,512]{1,0:T(8,128)(2,1)S(1)} %add_convert_fusion.9), channel_id=1, source_target_pairs={{0,1},{1,0},{2,3},{3,2},{4,5},{5,4},{6,7},{7,6},{8,9},{9,8},{10,11... | collective-permute-start | bytes 835592 | tf_op jit(solution)/shard_map/ppermute | solution.py:276
  106.4 17.2 %copy-start.55 = (f32[1024]{0:T(1024)}, f32[1024]{0:T(1024)S(1)}, u32[]{:S(2)}) copy-start(f32[1024]{0:T(1024)S(1)} %get-tuple-element.191) | copy-start | bytes 12292
  122.3 24.8 %collective-permute-start.7 = (bf16[1024,512]{1,0:T(8,128)(2,1)S(1)}, bf16[1024,512]{1,0:T(8,128)(2,1)S(1)}, u32[]{:S(2)}, u32[]{:S(2)}) collective-permute-start(bf16[1024,512]{1,0:T(8,128)(2,1)S(1)} %copy-done.33), channel_id=1, source_target_pairs={{0,16},{16,0},{1,17},{17,1},{2,18},{18,2},{3,19},{19,3},{4,20},{20... | collective-permute-start | bytes 3145736 | tf_op jit(solution)/shard_map/ppermute | solution.py:276
  124.5 25.9 %copy-start.14 = (f32[272,1024]{1,0:T(8,128)}, f32[272,1024]{1,0:T(8,128)S(1)}, u32[]{:S(2)}) copy-start(f32[272,1024]{1,0:T(8,128)S(1)} %convolution_add_fusion) | copy-start | bytes 3342340
  150.3 1.6 collective-permute-start.11
  151.3 2.3 collective-permute-start.8
  152.0 9.7 %collective-permute-start.12 = (bf16[272,512]{1,0:T(8,128)(2,1)S(1)}, bf16[272,512]{1,0:T(8,128)(2,1)}, u32[]{:S(2)}, u32[]{:S(2)}) collective-permute-start(bf16[272,512]{1,0:T(8,128)(2,1)S(1)} %add_convert_fusion.6), channel_id=1, source_target_pairs={{0,2},{1,3},{2,0},{3,1},{4,6},{5,7},{6,4},{7,5},{8,10},{9,11},{10,... | collective-permute-start | bytes 835592 | tf_op jit(solution)/shard_map/ppermute | solution.py:276
  154.4 13.7 %copy-start.53 = (bf16[512]{0:T(512)(128)(2,1)S(1)}, bf16[512]{0:T(512)(128)(2,1)}, u32[]{:S(2)}) copy-start(bf16[512]{0:T(512)(128)(2,1)} %get-tuple-element.161) | copy-start | bytes 3076
  154.4 13.7 %copy-start.66 = (bf16[512]{0:T(512)(128)(2,1)S(1)}, bf16[512]{0:T(512)(128)(2,1)}, u32[]{:S(2)}) copy-start(bf16[512]{0:T(512)(128)(2,1)} %param.25) | copy-start | bytes 3076
  154.4 12.5 %collective-permute-start.9 = (bf16[272,512]{1,0:T(8,128)(2,1)}, bf16[272,512]{1,0:T(8,128)(2,1)}, u32[]{:S(2)}, u32[]{:S(2)}) collective-permute-start(bf16[272,512]{1,0:T(8,128)(2,1)} %add_convert_fusion.8), channel_id=1, source_target_pairs={{0,2},{1,3},{2,0},{3,1},{4,6},{5,7},{6,4},{7,5},{8,10},{9,11},{10,... | collective-permute-start | bytes 835592 | tf_op jit(solution)/shard_map/ppermute | solution.py:276
  162.7 5.4 %collective-permute-start.13 = (bf16[272,512]{1,0:T(8,128)(2,1)S(1)}, bf16[272,512]{1,0:T(8,128)(2,1)S(1)}, u32[]{:S(2)}, u32[]{:S(2)}) collective-permute-start(bf16[272,512]{1,0:T(8,128)(2,1)S(1)} %add_convert_fusion.5), channel_id=1, source_target_pairs={{0,1},{1,0},{2,3},{3,2},{4,5},{5,4},{6,7},{7,6},{8,9},{9,8},{10,11... | collective-permute-start | bytes 835592 | tf_op jit(solution)/shard_map/ppermute | solution.py:276
  167.9 1.6 collective-permute-start.10
  168.1 3.6 copy-start.12
  175.1 11.4 %all-to-all-start.2 = ((bf16[4,272,64]{1,2,0:T(8,128)(2,1)}), bf16[4,272,64]{1,2,0:T(8,128)(2,1)S(1)}, u32[]{:S(2)}, u32[]{:S(2)}) async-start(bf16[4,272,64]{1,2,0:T(8,128)(2,1)} %bitcast.138), calls=%async_computation.2 | async-start | bytes 393216 | tf_op jit(solution)/shard_map/all_to_all | solution.py:438
  184.6 30.2 %collective-permute-start.20 = (bf16[1024,512]{1,0:T(8,128)(2,1)}, bf16[1024,512]{1,0:T(8,128)(2,1)}, u32[]{:S(2)}, u32[]{:S(2)}) collective-permute-start(bf16[1024,512]{1,0:T(8,128)(2,1)} %slice.410), channel_id=1, source_target_pairs={{0,16},{16,0},{1,17},{17,1},{2,18},{18,2},{3,19},{19,3},{4,20},{20... | collective-permute-start | bytes 3145736 | tf_op jit(solution)/shard_map/ppermute | solution.py:276
  188.2 5.5 %slice-start = ((s8[5013504]{0:T(1024)(128)(4,1)}), s8[819200]{0:T(1024)(128)(4,1)S(1)}, s32[]{:S(2)}) async-start(s8[5013504]{0:T(1024)(128)(4,1)} %bitcast.105), calls=%async_computation.8 | async-start | bytes 1638400
  190.1 3.7 slice-start.1
  203.0 4.6 %copy-start.56 = (f32[1024]{0:T(1024)S(1)}, f32[1024]{0:T(1024)}, u32[]{:S(2)}) copy-start(f32[1024]{0:T(1024)} %copy-done.55) | copy-start | bytes 12292
  204.1 18.3 %all-to-all-start.3 = ((bf16[4,272,192]{2,1,0:T(8,128)(2,1)}), bf16[4,272,192]{2,1,0:T(8,128)(2,1)S(1)}, u32[]{:S(2)}, u32[]{:S(2)}) async-start(bf16[4,272,192]{2,1,0:T(8,128)(2,1)} %copy.127), calls=%async_computation.3 | async-start | bytes 1114112 | tf_op jit(solution)/shard_map/all_to_all | solution.py:449
  207.6 62.3 %all-reduce.5.cloned.1.call-start = ((), (), s32[]{:S(2)}) async-start(), calls=%async_computation.4 | async-start | bytes 2097152 | tf_op jit(solution)/shard_map/psum | solution.py:425
  207.6 7.1 %copy-start.5 = (f32[1024,1024]{1,0:T(8,128)S(1)}, f32[1024,1024]{1,0:T(8,128)}, u32[]{:S(2)}) copy-start(f32[1024,1024]{1,0:T(8,128)} %copy-done.4) | copy-start | bytes 12582916
  213.4 24.5 %collective-permute-start.19 = (bf16[512,1024]{1,0:T(8,128)(2,1)}, bf16[512,1024]{1,0:T(8,128)(2,1)}, u32[]{:S(2)}, u32[]{:S(2)}) collective-permute-start(bf16[512,1024]{1,0:T(8,128)(2,1)} %slice.411), channel_id=1, source_target_pairs={{0,16},{16,0},{1,17},{17,1},{2,18},{18,2},{3,19},{19,3},{4,20},{20... | collective-permute-start | bytes 3145736 | tf_op jit(solution)/shard_map/ppermute | solution.py:276
  217.4 106.8 %all-reduce.7.cloned.1.call-start = ((), (), s32[]{:S(2)}) async-start(), calls=%async_computation.5 | async-start | bytes 2097152 | tf_op jit(solution)/shard_map/psum | solution.py:425
  222.8 3.1 copy-start.21
  224.2 3.9 copy-start.59
  224.2 4.5 %copy-start.49 = (f32[1024]{0:T(1024)S(1)}, f32[1024]{0:T(1024)}, u32[]{:S(2)}) copy-start(f32[1024]{0:T(1024)} %get-tuple-element.120) | copy-start | bytes 12292
  226.7 3.2 collective-permute-start.14
  231.7 38.7 %collective-permute-start.15 = (bf16[272,512]{1,0:T(8,128)(2,1)}, bf16[272,512]{1,0:T(8,128)(2,1)S(1)}, u32[]{:S(2)}, u32[]{:S(2)}) collective-permute-start(bf16[272,512]{1,0:T(8,128)(2,1)} %add_convert_fusion.4), channel_id=1, source_target_pairs={{0,2},{1,3},{2,0},{3,1},{4,6},{5,7},{6,4},{7,5},{8,10},{9,11},{10,... | collective-permute-start | bytes 835592 | tf_op jit(solution)/shard_map/ppermute | solution.py:276
  269.9 91.9 %all-reduce.9.cloned.1.call-start = ((), (), s32[]{:S(2)}) async-start(), calls=%async_computation.6 | async-start | bytes 524288 | tf_op jit(solution)/shard_map/psum | solution.py:425
  271.4 1.6 collective-permute-start.16
  279.5 44.7 %collective-permute-start.17 = (bf16[512,768]{1,0:T(8,128)(2,1)S(1)}, bf16[512,768]{1,0:T(8,128)(2,1)S(1)}, u32[]{:S(2)}, u32[]{:S(2)}) collective-permute-start(bf16[512,768]{1,0:T(8,128)(2,1)S(1)} %slice.412), channel_id=1, source_target_pairs={{0,16},{16,0},{1,17},{17,1},{2,18},{18,2},{3,19},{19,3},{4,20},{20... | collective-permute-start | bytes 2359304 | tf_op jit(solution)/shard_map/ppermute | solution.py:276
  281.0 4.2 copy-start.47
  281.1 5.4 %copy-start.46 = (f32[1024]{0:T(1024)S(1)}, f32[1024]{0:T(1024)}, u32[]{:S(2)}) copy-start(f32[1024]{0:T(1024)} %get-tuple-element.116) | copy-start | bytes 12292
  281.1 6.7 %copy-start.57 = (f32[256]{0:T(256)S(1)}, f32[256]{0:T(256)}, u32[]{:S(2)}) copy-start(f32[256]{0:T(256)} %reshape.699) | copy-start | bytes 3076
  281.1 8.0 %copy-start.58 = (f32[256]{0:T(256)S(1)}, f32[256]{0:T(256)}, u32[]{:S(2)}) copy-start(f32[256]{0:T(256)} %reshape.696) | copy-start | bytes 3076
  281.6 23.5 %collective-permute-start.18 = (bf16[256,512]{1,0:T(8,128)(2,1)S(1)}, bf16[256,512]{1,0:T(8,128)(2,1)S(1)}, u32[]{:S(2)}, u32[]{:S(2)}) collective-permute-start(bf16[256,512]{1,0:T(8,128)(2,1)S(1)} %slice.413), channel_id=1, source_target_pairs={{0,16},{16,0},{1,17},{17,1},{2,18},{18,2},{3,19},{19,3},{4,20},{20... | collective-permute-start | bytes 786440 | tf_op jit(solution)/shard_map/ppermute | solution.py:276
  324.2 84.3 %all-reduce.11.cloned.1.call-start = ((), (), s32[]{:S(2)}) async-start(), calls=%async_computation.7 | async-start | bytes 1572864 | tf_op jit(solution)/shard_map/psum | solution.py:425
  325.8 37.2 %copy-start.51 = (f32[4,256]{1,0:T(4,128)S(1)}, f32[4,256]{1,0:T(4,128)}, u32[]{:S(2)}) copy-start(f32[4,256]{1,0:T(4,128)} %reshape.697) | copy-start | bytes 12292
  325.8 43.9 %copy-start.24 = (bf16[272,1024]{1,0:T(8,128)(2,1)S(1)}, bf16[272,1024]{1,0:T(8,128)(2,1)}, u32[]{:S(2)}) copy-start(bf16[272,1024]{1,0:T(8,128)(2,1)} %get-tuple-element.129) | copy-start | bytes 1671172
  362.9 6.8 %copy-start.30 = (bf16[1024,512]{1,0:T(8,128)(2,1)S(1)}, bf16[1024,512]{1,0:T(8,128)(2,1)}, u32[]{:S(2)}) copy-start(bf16[1024,512]{1,0:T(8,128)(2,1)} %all-reduce.5.cloned.1.call-done) | copy-start | bytes 3145732
  364.3 3.9 collective-permute-start.21
  368.3 4.2 collective-permute-start.22
  369.7 4.4 %copy-start.18 = (bf16[272,512]{1,0:T(8,128)(2,1)S(1)}, bf16[272,512]{1,0:T(8,128)(2,1)}, u32[]{:S(2)}) copy-start(bf16[272,512]{1,0:T(8,128)(2,1)} %copy-done.17) | copy-start | bytes 835588
  369.8 4.4 %copy-start.20 = (bf16[272,512]{1,0:T(8,128)(2,1)S(1)}, bf16[272,512]{1,0:T(8,128)(2,1)}, u32[]{:S(2)}) copy-start(bf16[272,512]{1,0:T(8,128)(2,1)} %copy-done.19) | copy-start | bytes 835588
  372.4 5.5 %collective-permute-start.23 = (f32[3840]{0:T(1024)S(1)}, f32[3840]{0:T(1024)S(1)}, u32[]{:S(2)}, u32[]{:S(2)}) collective-permute-start(f32[3840]{0:T(1024)S(1)} %add.219), channel_id=1, source_target_pairs={{0,8},{4,12},{8,0},{12,4},{1,9},{5,13},{9,1},{13,5},{2,10},{6,14},... | collective-permute-start | bytes 46088 | tf_op jit(solution)/shard_map/ppermute | solution.py:276
  374.2 5.1 %copy-start.31 = (bf16[512,1024]{1,0:T(8,128)(2,1)S(1)}, bf16[512,1024]{1,0:T(8,128)(2,1)}, u32[]{:S(2)}) copy-start(bf16[512,1024]{1,0:T(8,128)(2,1)} %all-reduce.7.cloned.1.call-done) | copy-start | bytes 3145732
  (40 other events, 63.0 us)
Sparse Core Ops, SparseCore 0:
  217.5 52.3 all-reduce.4
  272.9 51.1 all-reduce.6
  327.1 34.6 all-reduce.8
  364.7 43.6 all-reduce.10

commit v2 on v1

--- a/solution.py
+++ b/solution.py
@@ -358,8 +358,7 @@
     flat_qkv = w_qkv.reshape(half, 3 * local)
     qkv_far = swap(flat_qkv, "fsdp", 1)
     out_far = swap(after(w_out, qkv_far), "fsdp", 1)
-    fc_far = swap(after(w_fc, out_far), "fsdp", 1)
-    proj_far = swap(after(w_proj, fc_far), "fsdp", 1)
+    fc_far = swap(after(w_fc, qkv_far), "fsdp", 1)
 
     def whole(index):
         far = packed_far[index * half : (index + 1) * half]
@@ -385,6 +384,7 @@
     seg_cols = jnp.broadcast_to(segments[0].astype(bf16)[None, :, None], (heads, rows, HD))
     send = jnp.concatenate((send, seg_cols), axis=2)
     got = lax.all_to_all(send, "context", 0, 0, tiled=True).reshape(heads * rows, 4 * HD)
+    proj_far = swap(after(w_proj, got), "fsdp", 1)
     queries, keys, values = got[:, :HD], got[:, HD : 2 * HD], got[:, 2 * HD : 3 * HD]
     seg_all = got[:, 3 * HD]
     position = jnp.arange(heads * rows, dtype=jnp.int32)
@@ -398,7 +398,9 @@
     pfull = exponent / row_total
     probs = pfull.astype(bf16)
     att_head = dot_to(probs, values, ((1,), (0,))).astype(bf16)
+    att_head, fc_far = lax.optimization_barrier((att_head, fc_far))
     att = lax.all_to_all(att_head.reshape(heads, rows, HD), "context", 0, 0, tiled=True)
+    att, proj_far = lax.optimization_barrier((att, proj_far))
     attended = jnp.transpose(att, (1, 0, 2)).reshape(rows, local)
 
     out_all = jnp.concatenate((w_out, out_far), axis=1)
@@ -413,21 +415,19 @@
     activ = activ.astype(bf16)
     grad_activ = dot_to(cot, proj_all, ((1,), (1,)))
     grad_pre = gelu_pull(grad_activ)[0].astype(bf16)
+    grad_proj = dot_to(activ, cot, ((0,), (0,)))
+    proj_send = grad_proj[:, half:].astype(bf16)
+    grad_pre, proj_send = lax.optimization_barrier((grad_pre, proj_send))
     grad_n2 = sum_four(dot_to(grad_pre, fc_all, ((1,), (1,))).astype(bf16))
     mlp_part = dot_to(activ, proj_all, ((1,), (0,))).astype(bf16)
     mixed = turn((hidden + sum_four(mlp_part) + bias_proj).astype(bf16))
 
-    def reduced(mine, theirs, earlier):
-        total = mine + swap(theirs.astype(bf16), "fsdp", 1).astype(f32)
-        total = total.astype(bf16)
-        if earlier is not None:
-            total = after(total, earlier)
-        return lax.psum(total, "context")
-
-    grad_proj = dot_to(activ, cot, ((0,), (0,)))
-    proj_sum = reduced(grad_proj[:, :half], grad_proj[:, half:], None)
+    def own_half(mine, theirs):
+        return (mine + swap(theirs.astype(bf16), "fsdp", 1).astype(f32)).astype(bf16)
+
+    proj_total = own_half(grad_proj[:, :half], proj_send)
     grad_fc = dot_to(normed2, grad_pre, ((0,), (0,)))
-    fc_sum = reduced(grad_fc[:half], grad_fc[half:], proj_sum)
+    fc_total = own_half(grad_fc[:half], grad_fc[half:])
 
     grad_out = cot.astype(f32)
     back_two, grad_gain_two, grad_shift_two = norm_back(grad_n2, nhat_two, rate_two, gain_two)
@@ -437,7 +437,9 @@
     grad_att = jnp.transpose(grad_att.reshape(rows, heads, HD), (1, 0, 2))
     grad_head = lax.all_to_all(grad_att, "context", 0, 0, tiled=True).reshape(heads * rows, HD)
     grad_w_out = dot_to(attended, grad_branch, ((0,), (0,)))
-    out_sum = reduced(grad_w_out[:, :half], grad_w_out[:, half:], fc_sum)
+    out_total = own_half(grad_w_out[:, :half], grad_w_out[:, half:])
+    grad_head, proj_total = lax.optimization_barrier((grad_head, proj_total))
+    proj_sum = lax.psum(proj_total, "context")
 
     grad_probs = dot_to(grad_head, values, ((1,), (1,)))
     row_delta = jnp.sum(grad_probs * pfull, axis=-1, keepdims=True)
@@ -446,11 +448,17 @@
     grad_k = SCORE_SCALE * dot_to(grad_scores, queries, ((0,), (0,)))
     grad_v = dot_to(probs, grad_head, ((0,), (0,)))
     back = jnp.concatenate((grad_q, grad_k, grad_v), axis=1).astype(bf16)
+    back, fc_total, out_total = lax.optimization_barrier((back, fc_total, out_total))
     back = lax.all_to_all(back.reshape(heads, rows, 3 * HD), "context", 0, 0, tiled=True)
     back = jnp.transpose(back.reshape(heads, rows, 3, HD), (1, 2, 0, 3)).reshape(rows, 3 * local)
+    grad_qkv = dot_to(normed1, back, ((0,), (0,)))
+    qkv_send = grad_qkv[half:].astype(bf16)
+    back, qkv_send = lax.optimization_barrier((back, qkv_send))
+    qkv_total = own_half(grad_qkv[:half], qkv_send)
     grad_n1 = sum_four(dot_to(back, qkv_all, ((1,), (1,))).astype(bf16))
-    grad_qkv = dot_to(normed1, back, ((0,), (0,)))
-    qkv_sum = reduced(grad_qkv[:half], grad_qkv[half:], out_sum)
+    last = lax.optimization_barrier((qkv_total, out_total, fc_total, proj_sum))
+    qkv_sum, out_sum, fc_sum = lax.psum(last[:3], "context")
+    proj_sum = last[3]
     back_one, grad_gain_one, grad_shift_one = norm_back(grad_n1, nhat_one, rate_one, gain_one)
     grad_tokens = turn(grad_hidden + back_one)
 

time: 419 us -> 361 us (0.86)
  waiting for transfers between devices: 236 us -> 203 us
  local copies, waits for them, and re-layouts: 61.5 us -> 46.6 us
  matrix products: 28.3 us -> 20.8 us
  other arithmetic: 40.3 us -> 35.9 us
    psum x4 -> x2, waiting for transfers between devices: 110 us -> 74.9 us  [the longest x1 71.8 us: fast_body(): qkv_sum, out_sum, fc_sum = lax.psum(last[:3], 'context')]
    all_to_all x1, waiting for transfers between devices: 5.04 us -> 19.5 us  [fast_body(): lax.all_to_all(back.reshape(heads, rows, 3 * HD), 'context', 0, 0, tiled=...]
    unnamed x165 -> x140, local copies, waits for them, and re-layouts: 34.3 us -> 20.9 us
    ppermute x24, waiting for transfers between devices: 100 us -> 90.8 us  [swap(): return lax.ppermute(values, axis, [(i, i ^ distance) for i in range(size)])]
    dot_general x18, matrix products: 28.3 us -> 20.8 us  [dot_to(): lax.dot_general(left, right, (dims, ((), ())), preferred_element_type=jnp...]
    mul x1 -> x0, local copies, waits for them, and re-layouts: 6.69 us -> none  [fast_body(): SCORE_SCALE * dot_to(queries, keys, ((1,), (1,)))]
    convert_element_type x5 -> x4, other arithmetic: 12.6 us -> 9.21 us  [own_half(): (mine + swap(theirs.astype(bf16), 'fsdp', 1).astype(f32)).astype(bf16)]
  transfers between devices with their start and end apart: 32 -> 30, of which waited for: 22 -> 22; matrix products, arithmetic and copies ran while one was open for 22% -> 19% of each run, Pallas kernels for 0% -> 0%
where the time goes in v2:
time: 361 us; the launch traced here: 360 us
  waiting for transfers between devices  203 us (56%)
  local copies, waits for them, and re-layouts  46.6 us (13%)
  starting transfers between devices  39 us (11%)
  other arithmetic  35.9 us (10%)
  matrix products  20.8 us (6%)
  between operations  15.1 us (4%)
    ppermute x24, waiting for transfers between devices, swap(): return lax.ppermute(values, axis, [(i, i ^ distance) for i in range(size)])  90.8 us
    psum x1, waiting for transfers between devices, fast_body(): qkv_sum, out_sum, fc_sum = lax.psum(last[:3], 'context')  71.8 us
    unnamed x140, local copies, waits for them, and re-layouts  20.9 us
    dot_general x18, matrix products, dot_to(): lax.dot_general(left, right, (dims, ((), ())), preferred_element_type=jnp...  20.8 us
    all_to_all x1, waiting for transfers between devices, fast_body(): lax.all_to_all(back.reshape(heads, rows, 3 * HD), 'context', 0, 0, tiled=...  19.5 us
    ppermute x24, starting transfers between devices, swap(): return lax.ppermute(values, axis, [(i, i ^ distance) for i in range(size)])  19 us
    all_to_all x1, waiting for transfers between devices, fast_body(): lax.all_to_all(send, 'context', 0, 0, tiled=True)  9.58 us
    convert_element_type x4, other arithmetic, own_half(): (mine + swap(theirs.astype(bf16), 'fsdp', 1).astype(f32)).astype(bf16)  9.21 us
  transfers between devices with their start and end apart: 30, of which 22 were waited for; matrix products, arithmetic and copies ran while one was open for 19% of the time, Pallas kernels for 0%

profile of v2, /device:TPU:0, one launch (start us, length us, event | category | flops | bytes accessed | tf_op | source)
XLA Modules:
  0.0 360.1 jit_solution(3619286792773235680)
XLA Ops:
  14.2 3.0 collective-permute-start
  17.2 1.4 copy.60
  21.4 16.3 %collective-permute-done.1 = bf16[512,768]{0,1:T(8,128)(2,1)S(1)} collective-permute-done((bf16[512,768]{0,1:T(8,128)(2,1)S(1)}, bf16[512,768]{0,1:T(8,128)(2,1)S(1)}, u32[]{:S(2)}, u32[]{:S(2)}) %collective-permute-start.1) | collective-permute-done | bytes 786464 | tf_op jit(solution)/shard_map/ppermute | solution.py:276
  40.2 4.9 %all-to-all-start = ((bf16[4,272,256]{2,1,0:T(8,128)(2,1)}), bf16[4,272,256]{2,1,0:T(8,128)(2,1)S(1)}, u32[]{:S(2)}, u32[]{:S(2)}) async-start(bf16[4,272,256]{2,1,0:T(8,128)(2,1)} %copy.63), calls=%async_computation | async-start | bytes 1114112 | tf_op jit(solution)/shard_map/all_to_all | solution.py:386
  48.0 1.5 collective-permute-start.2
  49.5 9.6 %all-to-all-done = bf16[4,272,256]{2,1,0:T(8,128)(2,1)S(1)} async-done(((bf16[4,272,256]{2,1,0:T(8,128)(2,1)}), bf16[4,272,256]{2,1,0:T(8,128)(2,1)S(1)}, u32[]{:S(2)}, u32[]{:S(2)}) %all-to-all-start) | async-done | bytes 557088 | tf_op jit(solution)/shard_map/all_to_all | solution.py:386
  59.9 1.2 fusion.96
  61.8 1.5 copy-done.1
  64.4 15.1 %collective-permute-done.2 = bf16[512,1024]{1,0:T(8,128)(2,1)} collective-permute-done((bf16[512,1024]{1,0:T(8,128)(2,1)S(1)}, bf16[512,1024]{1,0:T(8,128)(2,1)}, u32[]{:S(2)}, u32[]{:S(2)}) %collective-permute-start.2) | collective-permute-done | bytes 1048608 | tf_op jit(solution)/shard_map/ppermute | solution.py:276
  80.4 5.1 %all-to-all-start.1 = ((bf16[4,272,64]{1,2,0:T(8,128)(2,1)}), bf16[4,272,64]{1,2,0:T(8,128)(2,1)S(1)}, u32[]{:S(2)}, u32[]{:S(2)}) async-start(bf16[4,272,64]{1,2,0:T(8,128)(2,1)} %copy.64), calls=%async_computation.1 | async-start | bytes 393216 | tf_op jit(solution)/shard_map/all_to_all | solution.py:402
  86.5 5.2 %all-to-all-done.1 = bf16[4,272,64]{1,2,0:T(8,128)(2,1)S(1)} async-done(((bf16[4,272,64]{1,2,0:T(8,128)(2,1)}), bf16[4,272,64]{1,2,0:T(8,128)(2,1)S(1)}, u32[]{:S(2)}, u32[]{:S(2)}) %all-to-all-start.1) | async-done | bytes 139296 | tf_op jit(solution)/shard_map/all_to_all | solution.py:402
  91.7 7.5 %collective-permute-done.3 = bf16[1024,512]{1,0:T(8,128)(2,1)} collective-permute-done((bf16[1024,512]{1,0:T(8,128)(2,1)}, bf16[1024,512]{1,0:T(8,128)(2,1)}, u32[]{:S(2)}, u32[]{:S(2)}) %collective-permute-start.3) | collective-permute-done | bytes 1048608 | tf_op jit(solution)/shard_map/ppermute | solution.py:276
  101.6 1.3 constant_dynamic-update-slice_fusion.9
  104.0 1.6 collective-permute-start.6
  105.6 7.5 %collective-permute-done.6 = bf16[272,512]{1,0:T(8,128)(2,1)S(1)} collective-permute-done((bf16[272,512]{1,0:T(8,128)(2,1)S(1)}, bf16[272,512]{1,0:T(8,128)(2,1)S(1)}, u32[]{:S(2)}, u32[]{:S(2)}) %collective-permute-start.6) | collective-permute-done | bytes 278560 | tf_op jit(solution)/shard_map/ppermute | solution.py:276
  113.3 2.4 constant_dynamic-update-slice_fusion.2
  115.7 1.4 constant_dynamic-update-slice_fusion.4
  119.6 1.4 fusion.81
  121.0 1.5 fusion.46
  123.1 1.1 slice.425
  126.8 1.6 collective-permute-start.12
  128.3 3.4 fusion.84
  132.5 3.8 %collective-permute-done.12 = bf16[272,512]{1,0:T(8,128)(2,1)S(1)} collective-permute-done((bf16[272,512]{1,0:T(8,128)(2,1)S(1)}, bf16[272,512]{1,0:T(8,128)(2,1)S(1)}, u32[]{:S(2)}, u32[]{:S(2)}) %collective-permute-start.12) | collective-permute-done | bytes 278560 | tf_op jit(solution)/shard_map/ppermute | solution.py:276
  137.7 2.7 slice.424
  140.4 1.5 collective-permute-start.15
  143.1 1.2 fusion.50
  144.7 2.1 fusion.90
  148.0 4.8 %all-to-all-start.2 = ((bf16[4,272,64]{1,2,0:T(8,128)(2,1)}), bf16[4,272,64]{1,2,0:T(8,128)(2,1)S(1)}, u32[]{:S(2)}, u32[]{:S(2)}) async-start(bf16[4,272,64]{1,2,0:T(8,128)(2,1)} %bitcast.121), calls=%async_computation.2 | async-start | bytes 393216 | tf_op jit(solution)/shard_map/all_to_all | solution.py:438
  152.8 2.8 multiply_add_fusion.1
  158.0 2.7 all-to-all-done.2
  161.1 2.4 collective-permute-done.14
  163.5 3.2 fusion.7
  166.7 3.8 %multiply_reduce_fusion = (f32[1088]{0:T(1024)S(1)}, f32[1088,1088]{0,1:T(8,128)S(1)}) fusion(f32[1088]{0:T(1024)S(1)} %copy-done.32, f32[1088,1088]{0,1:T(8,128)} %copy-done.1, f32[1088]{0:T(1024)S(1)} %get-tuple-element.184, bf16[1088,64]{0,1:T(8,128)(2,1)S(1)} %reshape.694, bf16[1088,256]{1,0:T(8,128)(2,1)} %bitcast.106), kind=kOutput, calls=%fused_computation.3 | convolution fusion | flops 156253120 | bytes 10179328 | tf_op jit(solution)/shard_map/dot_general | solution.py:299
  173.7 12.3 %collective-permute-done.15 = bf16[512,1024]{1,0:T(8,128)(2,1)} collective-permute-done((bf16[512,1024]{1,0:T(8,128)(2,1)}, bf16[512,1024]{1,0:T(8,128)(2,1)}, u32[]{:S(2)}, u32[]{:S(2)}) %collective-permute-start.15) | collective-permute-done | bytes 1048608 | tf_op jit(solution)/shard_map/ppermute | solution.py:276
  186.0 2.5 fusion.6
  189.2 2.0 collective-permute-done.16
  191.2 1.7 fusion.70
  193.9 4.9 %all-to-all-start.3 = ((bf16[4,272,192]{2,1,0:T(8,128)(2,1)}), bf16[4,272,192]{2,1,0:T(8,128)(2,1)}, u32[]{:S(2)}, u32[]{:S(2)}) async-start(bf16[4,272,192]{2,1,0:T(8,128)(2,1)} %bitcast.115), calls=%async_computation.3 | async-start | bytes 1114112 | tf_op jit(solution)/shard_map/all_to_all | solution.py:452
  200.0 2.1 fusion.53
  202.5 19.5 %all-to-all-done.3 = bf16[4,272,192]{2,1,0:T(8,128)(2,1)} async-done(((bf16[4,272,192]{2,1,0:T(8,128)(2,1)}), bf16[4,272,192]{2,1,0:T(8,128)(2,1)}, u32[]{:S(2)}, u32[]{:S(2)}) %all-to-all-start.3) | async-done | bytes 417824 | tf_op jit(solution)/shard_map/all_to_all | solution.py:452
  222.0 2.1 copy.68
  224.1 1.1 copy.69
  225.3 1.2 fusion.55
  226.4 1.6 copy-done.4
  231.4 1.4 collective-permute-done.17
  232.8 1.1 add_convert_fusion.4
  233.9 1.5 collective-permute-start.18
  235.7 7.0 %collective-permute-done.18 = bf16[272,512]{1,0:T(8,128)(2,1)S(1)} collective-permute-done((bf16[272,512]{1,0:T(8,128)(2,1)S(1)}, bf16[272,512]{1,0:T(8,128)(2,1)S(1)}, u32[]{:S(2)}, u32[]{:S(2)}) %collective-permute-start.18) | collective-permute-done | bytes 278560 | tf_op jit(solution)/shard_map/ppermute | solution.py:276
  242.9 8.8 %collective-permute-done.20 = bf16[512,768]{1,0:T(8,128)(2,1)} collective-permute-done((bf16[512,768]{1,0:T(8,128)(2,1)}, bf16[512,768]{1,0:T(8,128)(2,1)}, u32[]{:S(2)}, u32[]{:S(2)}) %collective-permute-start.20) | collective-permute-done | bytes 786464 | tf_op jit(solution)/shard_map/ppermute | solution.py:276
  251.7 1.8 fusion.8
  253.5 3.1 all-reduce.4.cloned.1.call-done
  256.5 1.2 copy.70
  257.7 2.8 convert_element_type.386
  262.4 1.5 collective-permute-start.21
  264.3 1.8 collective-permute-done.21
  266.2 1.3 collective-permute-start.22
  267.6 2.6 collective-permute-done.22
  270.2 1.7 collective-permute-start.23
  271.9 1.5 fusion.38
  273.4 1.9 collective-permute-done.23
  276.6 71.8 %all-reduce.6.cloned.1.call-done = (bf16[512,3,256]{0,2,1:T(8,128)(2,1)}, bf16[256,512]{1,0:T(8,128)(2,1)}, bf16[512,1024]{1,0:T(8,128)(2,1)}) async-done(((bf16[512,3,256]{0,2,1:T(8,128)(2,1)}, bf16[256,512]{1,0:T(8,128)(2,1)}, bf16[512,1024]{1,0:T(8,128)(2,1)}), (bf16[512,3,256]{0,2,1:T(8,128)(2,1)}, bf16[256,512]{1,0:T(8,128)(2,1)}, bf16[512,1024]{1,0:T(8,128)(2,1)})) %all-reduce.6.cloned.1.call-update) | async-done | bytes 2097168 | tf_op jit(solution)/shard_map/psum | solution.py:460
  348.4 1.9 convert_element_type.384
  350.3 1.4 copy.71
  351.7 1.6 convert_element_type.385
  (266 shorter events, 49.5 us)
Async XLA Ops:
  7.2 11.5 %copy-start.8 = (bf16[1,272,1024]{2,1,0:T(8,128)(2,1)S(1)}, bf16[1,272,1024]{2,1,0:T(8,128)(2,1)}, u32[]{:S(2)}) copy-start(bf16[1,272,1024]{2,1,0:T(8,128)(2,1)} %param.15) | copy-start | bytes 1671172
  14.2 6.2 %collective-permute-start = (bf16[3840]{0:T(1024)(128)(2,1)S(1)}, bf16[3840]{0:T(1024)(128)(2,1)S(1)}, u32[]{:S(2)}, u32[]{:S(2)}) collective-permute-start(bf16[3840]{0:T(1024)(128)(2,1)S(1)} %dynamic-update-slice.31), channel_id=1, source_target_pairs={{0,16},{16,0},{1,17},{17,1},{2,18},{18,2},{3,19},{19,3},{4,20},{20... | collective-permute-start | bytes 23048 | tf_op jit(solution)/shard_map/ppermute | solution.py:276
  18.6 19.1 %copy-start.24 = (bf16[512,3,256]{0,2,1:T(8,128)(2,1)}, bf16[512,3,256]{0,2,1:T(8,128)(2,1)S(1)}, u32[]{:S(2)}) copy-start(bf16[512,3,256]{0,2,1:T(8,128)(2,1)S(1)} %copy.60) | copy-start | bytes 2359300
  18.6 19.1 %collective-permute-start.1 = (bf16[512,768]{0,1:T(8,128)(2,1)S(1)}, bf16[512,768]{0,1:T(8,128)(2,1)S(1)}, u32[]{:S(2)}, u32[]{:S(2)}) collective-permute-start(bf16[512,768]{0,1:T(8,128)(2,1)S(1)} %bitcast.118), channel_id=1, source_target_pairs={{0,16},{16,0},{1,17},{17,1},{2,18},{18,2},{3,19},{19,3},{4,20},{20... | collective-permute-start | bytes 2359304 | tf_op jit(solution)/shard_map/ppermute | solution.py:276
  21.4 17.0 %copy-start.33 = (f32[1024]{0:T(1024)}, f32[1024]{0:T(1024)S(1)}, u32[]{:S(2)}) copy-start(f32[1024]{0:T(1024)S(1)} %get-tuple-element.189) | copy-start | bytes 12292
  39.1 6.0 %copy-start.22 = (bf16[512,1024]{1,0:T(8,128)(2,1)S(1)}, bf16[512,1024]{1,0:T(8,128)(2,1)}, u32[]{:S(2)}) copy-start(bf16[512,1024]{1,0:T(8,128)(2,1)} %param.22) | copy-start | bytes 3145732
  40.2 18.9 %all-to-all-start = ((bf16[4,272,256]{2,1,0:T(8,128)(2,1)}), bf16[4,272,256]{2,1,0:T(8,128)(2,1)S(1)}, u32[]{:S(2)}, u32[]{:S(2)}) async-start(bf16[4,272,256]{2,1,0:T(8,128)(2,1)} %copy.63), calls=%async_computation | async-start | bytes 1114112 | tf_op jit(solution)/shard_map/all_to_all | solution.py:386
  47.4 39.1 %collective-permute-start.4 = (bf16[256,512]{1,0:T(8,128)(2,1)}, bf16[256,512]{1,0:T(8,128)(2,1)S(1)}, u32[]{:S(2)}, u32[]{:S(2)}) collective-permute-start(bf16[256,512]{1,0:T(8,128)(2,1)} %param.20), channel_id=1, source_target_pairs={{0,16},{16,0},{1,17},{17,1},{2,18},{18,2},{3,19},{19,3},{4,20},{20... | collective-permute-start | bytes 786440 | tf_op jit(solution)/shard_map/ppermute | solution.py:276
  48.0 31.5 %collective-permute-start.2 = (bf16[512,1024]{1,0:T(8,128)(2,1)S(1)}, bf16[512,1024]{1,0:T(8,128)(2,1)}, u32[]{:S(2)}, u32[]{:S(2)}) collective-permute-start(bf16[512,1024]{1,0:T(8,128)(2,1)S(1)} %copy-done.22), channel_id=1, source_target_pairs={{0,16},{16,0},{1,17},{17,1},{2,18},{18,2},{3,19},{19,3},{4,20},{20... | collective-permute-start | bytes 3145736 | tf_op jit(solution)/shard_map/ppermute | solution.py:276
  59.1 2.8 copy-start.10
  59.3 40.0 %collective-permute-start.3 = (bf16[1024,512]{1,0:T(8,128)(2,1)}, bf16[1024,512]{1,0:T(8,128)(2,1)}, u32[]{:S(2)}, u32[]{:S(2)}) collective-permute-start(bf16[1024,512]{1,0:T(8,128)(2,1)} %param.24), channel_id=1, source_target_pairs={{0,16},{16,0},{1,17},{17,1},{2,18},{18,2},{3,19},{19,3},{4,20},{20... | collective-permute-start | bytes 3145736 | tf_op jit(solution)/shard_map/ppermute | solution.py:276
  61.1 2.3 copy-start.1
  80.4 11.3 %all-to-all-start.1 = ((bf16[4,272,64]{1,2,0:T(8,128)(2,1)}), bf16[4,272,64]{1,2,0:T(8,128)(2,1)S(1)}, u32[]{:S(2)}, u32[]{:S(2)}) async-start(bf16[4,272,64]{1,2,0:T(8,128)(2,1)} %copy.64), calls=%async_computation.1 | async-start | bytes 393216 | tf_op jit(solution)/shard_map/all_to_all | solution.py:402
  86.5 15.0 %copy-start.12 = (bf16[256,1024]{1,0:T(8,128)(2,1)}, bf16[256,1024]{1,0:T(8,128)(2,1)S(1)}, u32[]{:S(2)}) copy-start(bf16[256,1024]{1,0:T(8,128)(2,1)S(1)} %constant_dynamic-update-slice_fusion) | copy-start | bytes 1572868
  86.5 14.0 %copy-start.23 = (bf16[1024,512]{1,0:T(8,128)(2,1)S(1)}, bf16[1024,512]{1,0:T(8,128)(2,1)}, u32[]{:S(2)}) copy-start(bf16[1024,512]{1,0:T(8,128)(2,1)} %param.24) | copy-start | bytes 3145732
  100.4 5.2 %copy-start.45 = (bf16[512]{0:T(512)(128)(2,1)S(1)}, bf16[512]{0:T(512)(128)(2,1)}, u32[]{:S(2)}) copy-start(bf16[512]{0:T(512)(128)(2,1)} %get-tuple-element.157) | copy-start | bytes 3076
  100.4 5.2 %copy-start.50 = (bf16[512]{0:T(512)(128)(2,1)S(1)}, bf16[512]{0:T(512)(128)(2,1)}, u32[]{:S(2)}) copy-start(bf16[512]{0:T(512)(128)(2,1)} %param.25) | copy-start | bytes 3076
  100.4 5.2 %copy-start.44 = (bf16[512]{0:T(512)(128)(2,1)S(1)}, bf16[512]{0:T(512)(128)(2,1)}, u32[]{:S(2)}) copy-start(bf16[512]{0:T(512)(128)(2,1)} %get-tuple-element.161) | copy-start | bytes 3076
  100.4 5.2 %copy-start.51 = (bf16[512]{0:T(512)(128)(2,1)S(1)}, bf16[512]{0:T(512)(128)(2,1)}, u32[]{:S(2)}) copy-start(bf16[512]{0:T(512)(128)(2,1)} %param.21) | copy-start | bytes 3076
  100.4 5.2 %copy-start.41 = (bf16[512]{0:T(512)(128)(2,1)S(1)}, bf16[512]{0:T(512)(128)(2,1)}, u32[]{:S(2)}) copy-start(bf16[512]{0:T(512)(128)(2,1)} %get-tuple-element.159) | copy-start | bytes 3076
  100.4 5.2 %copy-start.42 = (bf16[512]{0:T(512)(128)(2,1)S(1)}, bf16[512]{0:T(512)(128)(2,1)}, u32[]{:S(2)}) copy-start(bf16[512]{0:T(512)(128)(2,1)} %get-tuple-element.160) | copy-start | bytes 3076
  100.4 5.2 %copy-start.48 = (bf16[512]{0:T(512)(128)(2,1)S(1)}, bf16[512]{0:T(512)(128)(2,1)}, u32[]{:S(2)}) copy-start(bf16[512]{0:T(512)(128)(2,1)} %param.28) | copy-start | bytes 3076
  100.4 5.2 %copy-start.49 = (bf16[512]{0:T(512)(128)(2,1)S(1)}, bf16[512]{0:T(512)(128)(2,1)}, u32[]{:S(2)}) copy-start(bf16[512]{0:T(512)(128)(2,1)} %param.29) | copy-start | bytes 3076
  100.4 2.5 collective-permute-start.5
  101.6 11.7 %copy-start.43 = (bf16[4,128]{1,0:T(4,128)(2,1)S(1)}, bf16[4,128]{1,0:T(4,128)(2,1)}, u32[]{:S(2)}) copy-start(bf16[4,128]{1,0:T(4,128)(2,1)} %get-tuple-element.158) | copy-start | bytes 3076
  101.6 11.7 %copy-start.52 = (bf16[4,128]{1,0:T(4,128)(2,1)S(1)}, bf16[4,128]{1,0:T(4,128)(2,1)}, u32[]{:S(2)}) copy-start(bf16[4,128]{1,0:T(4,128)(2,1)} %param.23) | copy-start | bytes 3076
  104.0 9.1 %collective-permute-start.6 = (bf16[272,512]{1,0:T(8,128)(2,1)S(1)}, bf16[272,512]{1,0:T(8,128)(2,1)S(1)}, u32[]{:S(2)}, u32[]{:S(2)}) collective-permute-start(bf16[272,512]{1,0:T(8,128)(2,1)S(1)} %add_convert_fusion.10), channel_id=1, source_target_pairs={{0,2},{1,3},{2,0},{3,1},{4,6},{5,7},{6,4},{7,5},{8,10},{9,11},{10,... | collective-permute-start | bytes 835592 | tf_op jit(solution)/shard_map/ppermute | solution.py:276
  113.2 2.5 copy-start.28
  113.2 3.9 %collective-permute-start.7 = (bf16[272,512]{1,0:T(8,128)(2,1)S(1)}, bf16[272,512]{1,0:T(8,128)(2,1)S(1)}, u32[]{:S(2)}, u32[]{:S(2)}) collective-permute-start(bf16[272,512]{1,0:T(8,128)(2,1)S(1)} %add_convert_fusion.9), channel_id=1, source_target_pairs={{0,1},{1,0},{2,3},{3,2},{4,5},{5,4},{6,7},{7,6},{8,9},{9,8},{10,11... | collective-permute-start | bytes 835592 | tf_op jit(solution)/shard_map/ppermute | solution.py:276
  125.1 1.6 collective-permute-start.11
  126.4 5.4 %collective-permute-start.8 = (bf16[272,512]{1,0:T(8,128)(2,1)S(1)}, bf16[272,512]{1,0:T(8,128)(2,1)S(1)}, u32[]{:S(2)}, u32[]{:S(2)}) collective-permute-start(bf16[272,512]{1,0:T(8,128)(2,1)S(1)} %broadcast_select_fusion.8), channel_id=1, source_target_pairs={{0,1},{1,0},{2,3},{3,2},{4,5},{5,4},{6,7},{7,6},{8,9},{9,8},{10,11... | collective-permute-start | bytes 835592 | tf_op jit(solution)/shard_map/ppermute | solution.py:276
  126.8 9.6 %collective-permute-start.12 = (bf16[272,512]{1,0:T(8,128)(2,1)S(1)}, bf16[272,512]{1,0:T(8,128)(2,1)S(1)}, u32[]{:S(2)}, u32[]{:S(2)}) collective-permute-start(bf16[272,512]{1,0:T(8,128)(2,1)S(1)} %add_convert_fusion.6), channel_id=1, source_target_pairs={{0,2},{1,3},{2,0},{3,1},{4,6},{5,7},{6,4},{7,5},{8,10},{9,11},{10,... | collective-permute-start | bytes 835592 | tf_op jit(solution)/shard_map/ppermute | solution.py:276
  131.9 10.1 %collective-permute-start.9 = (bf16[272,512]{1,0:T(8,128)(2,1)S(1)}, bf16[272,512]{1,0:T(8,128)(2,1)}, u32[]{:S(2)}, u32[]{:S(2)}) collective-permute-start(bf16[272,512]{1,0:T(8,128)(2,1)S(1)} %add_convert_fusion.8), channel_id=1, source_target_pairs={{0,2},{1,3},{2,0},{3,1},{4,6},{5,7},{6,4},{7,5},{8,10},{9,11},{10,... | collective-permute-start | bytes 835592 | tf_op jit(solution)/shard_map/ppermute | solution.py:276
  136.4 6.7 %collective-permute-start.13 = (bf16[272,512]{1,0:T(8,128)(2,1)S(1)}, bf16[272,512]{1,0:T(8,128)(2,1)S(1)}, u32[]{:S(2)}, u32[]{:S(2)}) collective-permute-start(bf16[272,512]{1,0:T(8,128)(2,1)S(1)} %add_convert_fusion.5), channel_id=1, source_target_pairs={{0,1},{1,0},{2,3},{3,2},{4,5},{5,4},{6,7},{7,6},{8,9},{9,8},{10,11... | collective-permute-start | bytes 835592 | tf_op jit(solution)/shard_map/ppermute | solution.py:276
  137.2 26.3 %collective-permute-start.14 = (bf16[1024,512]{1,0:T(8,128)(2,1)}, bf16[1024,512]{1,0:T(8,128)(2,1)}, u32[]{:S(2)}, u32[]{:S(2)}) collective-permute-start(bf16[1024,512]{1,0:T(8,128)(2,1)} %slice.425), channel_id=1, source_target_pairs={{0,16},{16,0},{1,17},{17,1},{2,18},{18,2},{3,19},{19,3},{4,20},{20... | collective-permute-start | bytes 3145736 | tf_op jit(solution)/shard_map/ppermute | solution.py:276
  140.4 45.5 %collective-permute-start.15 = (bf16[512,1024]{1,0:T(8,128)(2,1)}, bf16[512,1024]{1,0:T(8,128)(2,1)}, u32[]{:S(2)}, u32[]{:S(2)}) collective-permute-start(bf16[512,1024]{1,0:T(8,128)(2,1)} %slice.424), channel_id=1, source_target_pairs={{0,16},{16,0},{1,17},{17,1},{2,18},{18,2},{3,19},{19,3},{4,20},{20... | collective-permute-start | bytes 3145736 | tf_op jit(solution)/shard_map/ppermute | solution.py:276
  143.0 1.6 collective-permute-start.10
  144.7 2.2 copy-start.16
  146.9 6.0 %copy-start.7 = (bf16[1,272,1024]{2,1,0:T(8,128)(2,1)S(1)}, bf16[1,272,1024]{2,1,0:T(8,128)(2,1)}, u32[]{:S(2)}) copy-start(bf16[1,272,1024]{2,1,0:T(8,128)(2,1)} %param.17) | copy-start | bytes 1671172
  148.0 12.7 %all-to-all-start.2 = ((bf16[4,272,64]{1,2,0:T(8,128)(2,1)}), bf16[4,272,64]{1,2,0:T(8,128)(2,1)S(1)}, u32[]{:S(2)}, u32[]{:S(2)}) async-start(bf16[4,272,64]{1,2,0:T(8,128)(2,1)} %bitcast.121), calls=%async_computation.2 | async-start | bytes 393216 | tf_op jit(solution)/shard_map/all_to_all | solution.py:438
  157.6 33.5 %collective-permute-start.16 = (bf16[256,512]{1,0:T(8,128)(2,1)S(1)}, bf16[256,512]{1,0:T(8,128)(2,1)}, u32[]{:S(2)}, u32[]{:S(2)}) collective-permute-start(bf16[256,512]{1,0:T(8,128)(2,1)S(1)} %slice.427), channel_id=1, source_target_pairs={{0,16},{16,0},{1,17},{17,1},{2,18},{18,2},{3,19},{19,3},{4,20},{20... | collective-permute-start | bytes 786440 | tf_op jit(solution)/shard_map/ppermute | solution.py:276
  161.1 5.6 %copy-start.29 = (bf16[1088,64]{0,1:T(8,128)(2,1)}, bf16[1088,64]{0,1:T(8,128)(2,1)S(1)}, u32[]{:S(2)}) copy-start(bf16[1088,64]{0,1:T(8,128)(2,1)S(1)} %reshape.694) | copy-start | bytes 417796
  161.1 5.6 %copy-start.32 = (f32[1088]{0:T(1024)S(1)}, f32[1088]{0:T(1024)}, u32[]{:S(2)}) copy-start(f32[1088]{0:T(1024)} %copy-done.31) | copy-start | bytes 13060
  166.7 3.8 %slice-start = ((s8[5013504]{0:T(1024)(128)(4,1)}), s8[819200]{0:T(1024)(128)(4,1)S(1)}, s32[]{:S(2)}) async-start(s8[5013504]{0:T(1024)(128)(4,1)} %bitcast.88), calls=%async_computation.6 | async-start | bytes 1638400
  166.7 4.0 %slice-start.1 = ((s8[5013504]{0:T(1024)(128)(4,1)}), s8[4194304]{0:T(1024)(128)(4,1)S(1)}, s32[]{:S(2)}) async-start(s8[5013504]{0:T(1024)(128)(4,1)} %bitcast.88), calls=%async_computation.7 | async-start | bytes 8388608
  172.7 13.3 %copy-start.19 = (f32[1024,1024]{1,0:T(8,128)S(1)}, f32[1024,1024]{1,0:T(8,128)}, u32[]{:S(2)}) copy-start(f32[1024,1024]{1,0:T(8,128)} %fusion.84) | copy-start | bytes 12582916
  188.5 2.7 copy-start.15
  192.9 6.0 %copy-start.37 = (f32[3840]{0:T(1024)S(1)}, f32[3840]{0:T(1024)}, u32[]{:S(2)}) copy-start(f32[3840]{0:T(1024)} %get-tuple-element.179) | copy-start | bytes 46084
  192.9 6.0 %copy-start.39 = (f32[1024]{0:T(1024)S(1)}, f32[1024]{0:T(1024)}, u32[]{:S(2)}) copy-start(f32[1024]{0:T(1024)} %get-tuple-element.121) | copy-start | bytes 12292
  192.9 6.0 %copy-start.56 = (f32[3840]{0:T(1024)S(1)}, f32[3840]{0:T(1024)}, u32[]{:S(2)}) copy-start(f32[3840]{0:T(1024)} %get-tuple-element.178) | copy-start | bytes 46084
  193.9 6.0 %copy-start.5 = (bf16[1,272,1024]{2,1,0:T(8,128)(2,1)S(1)}, bf16[1,272,1024]{2,1,0:T(8,128)(2,1)}, u32[]{:S(2)}) copy-start(bf16[1,272,1024]{2,1,0:T(8,128)(2,1)} %get-tuple-element.126) | copy-start | bytes 1671172
  193.9 6.1 %copy-start.17 = (bf16[272,512]{1,0:T(8,128)(2,1)S(1)}, bf16[272,512]{1,0:T(8,128)(2,1)}, u32[]{:S(2)}) copy-start(bf16[272,512]{1,0:T(8,128)(2,1)} %copy-done.16) | copy-start | bytes 835588
  193.9 28.0 %all-to-all-start.3 = ((bf16[4,272,192]{2,1,0:T(8,128)(2,1)}), bf16[4,272,192]{2,1,0:T(8,128)(2,1)}, u32[]{:S(2)}, u32[]{:S(2)}) async-start(bf16[4,272,192]{2,1,0:T(8,128)(2,1)} %bitcast.115), calls=%async_computation.3 | async-start | bytes 1114112 | tf_op jit(solution)/shard_map/all_to_all | solution.py:452
  198.9 57.7 %all-reduce.4.cloned.1.call-start = ((), (), s32[]{:S(2)}) async-start(), calls=%async_computation.4 | async-start | bytes 2097152 | tf_op jit(solution)/shard_map/psum | solution.py:442
  202.1 23.1 %copy-start.34 = (f32[1024]{0:T(1024)S(1)}, f32[1024]{0:T(1024)}, u32[]{:S(2)}) copy-start(f32[1024]{0:T(1024)} %copy-done.33) | copy-start | bytes 12292
  202.2 146.2 %all-reduce.6.cloned.1.call-start = ((), (), s32[]{:S(2)}) async-start(), calls=%async_computation.5 | async-start | bytes 4194304 | tf_op jit(solution)/shard_map/psum | solution.py:460
  231.2 1.6 collective-permute-start.17
  231.4 20.3 %collective-permute-start.20 = (bf16[512,768]{1,0:T(8,128)(2,1)}, bf16[512,768]{1,0:T(8,128)(2,1)}, u32[]{:S(2)}, u32[]{:S(2)}) collective-permute-start(bf16[512,768]{1,0:T(8,128)(2,1)} %slice.426), channel_id=1, source_target_pairs={{0,16},{16,0},{1,17},{17,1},{2,18},{18,2},{3,19},{19,3},{4,20},{20... | collective-permute-start | bytes 2359304 | tf_op jit(solution)/shard_map/ppermute | solution.py:276
  233.9 8.8 %collective-permute-start.18 = (bf16[272,512]{1,0:T(8,128)(2,1)S(1)}, bf16[272,512]{1,0:T(8,128)(2,1)S(1)}, u32[]{:S(2)}, u32[]{:S(2)}) collective-permute-start(bf16[272,512]{1,0:T(8,128)(2,1)S(1)} %add_convert_fusion.4), channel_id=1, source_target_pairs={{0,2},{1,3},{2,0},{3,1},{4,6},{5,7},{6,4},{7,5},{8,10},{9,11},{10,... | collective-permute-start | bytes 835592 | tf_op jit(solution)/shard_map/ppermute | solution.py:276
  242.8 17.8 %collective-permute-start.19 = (bf16[272,512]{1,0:T(8,128)(2,1)S(1)}, bf16[272,512]{1,0:T(8,128)(2,1)}, u32[]{:S(2)}, u32[]{:S(2)}) collective-permute-start(bf16[272,512]{1,0:T(8,128)(2,1)S(1)} %add_convert_fusion.3), channel_id=1, source_target_pairs={{0,1},{1,0},{2,3},{3,2},{4,5},{5,4},{6,7},{7,6},{8,9},{9,8},{10,11... | collective-permute-start | bytes 835592 | tf_op jit(solution)/shard_map/ppermute | solution.py:276
  262.4 3.8 %collective-permute-start.21 = (f32[3840]{0:T(1024)S(1)}, f32[3840]{0:T(1024)S(1)}, u32[]{:S(2)}, u32[]{:S(2)}) collective-permute-start(f32[3840]{0:T(1024)S(1)} %get-tuple-element.164), channel_id=1, source_target_pairs={{0,16},{16,0},{1,17},{17,1},{2,18},{18,2},{3,19},{19,3},{4,20},{20... | collective-permute-start | bytes 46088 | tf_op jit(solution)/shard_map/ppermute | solution.py:276
  266.2 5.8 %copy-start.3 = (f32[1,272,1024]{2,1,0:T(8,128)S(1)}, f32[1,272,1024]{2,1,0:T(8,128)}, u32[]{:S(2)}) copy-start(f32[1,272,1024]{2,1,0:T(8,128)} %copy-done.2) | copy-start | bytes 3342340
  266.2 4.1 %collective-permute-start.22 = (f32[3840]{0:T(1024)S(1)}, f32[3840]{0:T(1024)S(1)}, u32[]{:S(2)}, u32[]{:S(2)}) collective-permute-start(f32[3840]{0:T(1024)S(1)} %add.218), channel_id=1, source_target_pairs={{0,4},{4,0},{8,12},{12,8},{1,5},{5,1},{9,13},{13,9},{2,6},{6,2},{1... | collective-permute-start | bytes 46088 | tf_op jit(solution)/shard_map/ppermute | solution.py:276
  270.2 5.1 %collective-permute-start.23 = (f32[3840]{0:T(1024)S(1)}, f32[3840]{0:T(1024)S(1)}, u32[]{:S(2)}, u32[]{:S(2)}) collective-permute-start(f32[3840]{0:T(1024)S(1)} %add.219), channel_id=1, source_target_pairs={{0,8},{4,12},{8,0},{12,4},{1,9},{5,13},{9,1},{13,5},{2,10},{6,14},... | collective-permute-start | bytes 46088 | tf_op jit(solution)/shard_map/ppermute | solution.py:276
  (25 other events, 35.5 us)
Sparse Core Ops, SparseCore 0:
  202.3 54.2 all-reduce.3
  260.7 87.6 all-reduce.5

commit v3 on v2

--- a/solution.py
+++ b/solution.py
@@ -398,19 +398,19 @@
     pfull = exponent / row_total
     probs = pfull.astype(bf16)
     att_head = dot_to(probs, values, ((1,), (0,))).astype(bf16)
-    att_head, fc_far = lax.optimization_barrier((att_head, fc_far))
     att = lax.all_to_all(att_head.reshape(heads, rows, HD), "context", 0, 0, tiled=True)
-    att, proj_far = lax.optimization_barrier((att, proj_far))
+    att, fc_far = lax.optimization_barrier((att, fc_far))
     attended = jnp.transpose(att, (1, 0, 2)).reshape(rows, local)
 
     out_all = jnp.concatenate((w_out, out_far), axis=1)
     attn_part = dot_to(attended, out_all, ((1,), (0,))).astype(bf16)
-    hidden = base + sum_four(attn_part) + bias_out
+    attn_sum, proj_far = lax.optimization_barrier((sum_four(attn_part), proj_far))
+    hidden = base + attn_sum + bias_out
     nhat_two, rate_two = norm_parts(hidden)
     normed2 = (nhat_two * gain_two + shift_two).astype(bf16)
     fc_all = jnp.concatenate((w_fc, fc_far), axis=0)
+    pre_act = dot_to(normed2, fc_all, ((1,), (0,))) + bias_fc
     proj_all = jnp.concatenate((w_proj, proj_far), axis=1)
-    pre_act = dot_to(normed2, fc_all, ((1,), (0,))) + bias_fc
     activ, gelu_pull = jax.vjp(gelu_tanh, pre_act)
     activ = activ.astype(bf16)
     grad_activ = dot_to(cot, proj_all, ((1,), (1,)))
@@ -448,9 +448,9 @@
     grad_k = SCORE_SCALE * dot_to(grad_scores, queries, ((0,), (0,)))
     grad_v = dot_to(probs, grad_head, ((0,), (0,)))
     back = jnp.concatenate((grad_q, grad_k, grad_v), axis=1).astype(bf16)
-    back, fc_total, out_total = lax.optimization_barrier((back, fc_total, out_total))
     back = lax.all_to_all(back.reshape(heads, rows, 3 * HD), "context", 0, 0, tiled=True)
     back = jnp.transpose(back.reshape(heads, rows, 3, HD), (1, 2, 0, 3)).reshape(rows, 3 * local)
+    back, fc_total, out_total = lax.optimization_barrier((back, fc_total, out_total))
     grad_qkv = dot_to(normed1, back, ((0,), (0,)))
     qkv_send = grad_qkv[half:].astype(bf16)
     back, qkv_send = lax.optimization_barrier((back, qkv_send))

time: 361 us -> 341 us (0.945)
  waiting for transfers between devices: 203 us -> 192 us
  local copies, waits for them, and re-layouts: 46.6 us -> 36.8 us
  matrix products: 20.8 us -> 25 us
    ppermute x24, waiting for transfers between devices: 90.8 us -> 75.1 us  [swap(): return lax.ppermute(values, axis, [(i, i ^ distance) for i in range(size)])]
    psum x1, waiting for transfers between devices: 3.08 us -> 7.43 us  [fast_body(): proj_sum = lax.psum(proj_total, 'context')]
    dot_general x18, matrix products: 20.8 us -> 25 us  [dot_to(): lax.dot_general(left, right, (dims, ((), ())), preferred_element_type=jnp...]
    unnamed x140 -> x118, local copies, waits for them, and re-layouts: 20.9 us -> 20 us
  transfers between devices with their start and end apart: 30 -> 30, of which waited for: 22 -> 20; matrix products, arithmetic and copies ran while one was open for 19% -> 20% of each run, Pallas kernels for 0% -> 0%
where the time goes in v3:
time: 341 us; the launch traced here: 340 us
  waiting for transfers between devices  192 us (56%)
  local copies, waits for them, and re-layouts  36.8 us (11%)
  starting transfers between devices  35.8 us (10%)
  other arithmetic  34.6 us (10%)
  matrix products  25 us (7%)
  between operations  15.1 us (4%)
    ppermute x24, waiting for transfers between devices, swap(): return lax.ppermute(values, axis, [(i, i ^ distance) for i in range(size)])  75.1 us
    psum x1, waiting for transfers between devices, fast_body(): qkv_sum, out_sum, fc_sum = lax.psum(last[:3], 'context')  72 us
    dot_general x18, matrix products, dot_to(): lax.dot_general(left, right, (dims, ((), ())), preferred_element_type=jnp...  25 us
    unnamed x118, local copies, waits for them, and re-layouts  20 us
    ppermute x24, starting transfers between devices, swap(): return lax.ppermute(values, axis, [(i, i ^ distance) for i in range(size)])  17.7 us
    all_to_all x1, waiting for transfers between devices, fast_body(): lax.all_to_all(back.reshape(heads, rows, 3 * HD), 'context', 0, 0, tiled=...  16.8 us
    all_to_all x1, waiting for transfers between devices, fast_body(): lax.all_to_all(send, 'context', 0, 0, tiled=True)  11.7 us
    convert_element_type x4, other arithmetic, own_half(): (mine + swap(theirs.astype(bf16), 'fsdp', 1).astype(f32)).astype(bf16)  9.64 us
  transfers between devices with their start and end apart: 30, of which 20 were waited for; matrix products, arithmetic and copies ran while one was open for 20% of the time, Pallas kernels for 0%

profile of v3, /device:TPU:0, one launch (start us, length us, event | category | flops | bytes accessed | tf_op | source)
XLA Modules:
  0.0 339.6 jit_solution(16179004981497782509)
XLA Ops:
  14.2 3.0 collective-permute-start
  17.2 1.4 copy.51
  20.0 17.7 %collective-permute-done.1 = bf16[512,768]{0,1:T(8,128)(2,1)S(1)} collective-permute-done((bf16[512,768]{0,1:T(8,128)(2,1)S(1)}, bf16[512,768]{0,1:T(8,128)(2,1)S(1)}, u32[]{:S(2)}, u32[]{:S(2)}) %collective-permute-start.1) | collective-permute-done | bytes 786464 | tf_op jit(solution)/shard_map/ppermute | solution.py:276
  39.1 1.1 copy.54
  40.2 4.9 %all-to-all-start = ((bf16[4,272,256]{2,1,0:T(8,128)(2,1)}), bf16[4,272,256]{2,1,0:T(8,128)(2,1)S(1)}, u32[]{:S(2)}, u32[]{:S(2)}) async-start(bf16[4,272,256]{2,1,0:T(8,128)(2,1)} %copy.54), calls=%async_computation | async-start | bytes 1114112 | tf_op jit(solution)/shard_map/all_to_all | solution.py:386
  45.9 1.5 collective-permute-start.2
  47.4 11.7 %all-to-all-done = bf16[4,272,256]{2,1,0:T(8,128)(2,1)S(1)} async-done(((bf16[4,272,256]{2,1,0:T(8,128)(2,1)}), bf16[4,272,256]{2,1,0:T(8,128)(2,1)S(1)}, u32[]{:S(2)}, u32[]{:S(2)}) %all-to-all-start) | async-done | bytes 557088 | tf_op jit(solution)/shard_map/all_to_all | solution.py:386
  59.4 1.2 fusion.79
  61.3 1.5 copy-done.1
  64.7 3.5 %all-to-all-start.1 = ((bf16[4,272,64]{1,2,0:T(8,128)(2,1)}), bf16[4,272,64]{1,2,0:T(8,128)(2,1)S(1)}, u32[]{:S(2)}, u32[]{:S(2)}) async-start(bf16[4,272,64]{1,2,0:T(8,128)(2,1)} %copy.55), calls=%async_computation.1 | async-start | bytes 393216 | tf_op jit(solution)/shard_map/all_to_all | solution.py:401
  70.3 4.5 %all-to-all-done.1 = bf16[4,272,64]{1,2,0:T(8,128)(2,1)S(1)} async-done(((bf16[4,272,64]{1,2,0:T(8,128)(2,1)}), bf16[4,272,64]{1,2,0:T(8,128)(2,1)S(1)}, u32[]{:S(2)}, u32[]{:S(2)}) %all-to-all-start.1) | async-done | bytes 139296 | tf_op jit(solution)/shard_map/all_to_all | solution.py:401
  75.9 2.3 constant_dynamic-update-slice_fusion.3
  78.1 1.3 constant_dynamic-update-slice_fusion.9
  79.4 1.1 add_convert_fusion.9
  80.6 1.6 collective-permute-start.5
  82.1 1.4 constant_dynamic-update-slice_fusion.5
  84.6 5.1 %collective-permute-done.5 = bf16[272,512]{1,0:T(8,128)(2,1)S(1)} collective-permute-done((bf16[272,512]{1,0:T(8,128)(2,1)S(1)}, bf16[272,512]{1,0:T(8,128)(2,1)S(1)}, u32[]{:S(2)}, u32[]{:S(2)}) %collective-permute-start.5) | collective-permute-done | bytes 278560 | tf_op jit(solution)/shard_map/ppermute | solution.py:276
  90.0 1.4 collective-permute-done.6
  91.6 18.0 %collective-permute-done.7 = bf16[1024,512]{1,0:T(8,128)(2,1)S(1)} collective-permute-done((bf16[1024,512]{1,0:T(8,128)(2,1)}, bf16[1024,512]{1,0:T(8,128)(2,1)S(1)}, u32[]{:S(2)}, u32[]{:S(2)}) %collective-permute-start.7) | collective-permute-done | bytes 1048608 | tf_op jit(solution)/shard_map/ppermute | solution.py:276
  111.2 1.4 fusion.62
  112.6 1.5 fusion.36
  114.7 1.1 slice.417
  119.2 3.5 %fusion.65 = f32[1024,1024]{1,0:T(8,128)} fusion(bf16[272,1024]{1,0:T(8,128)(2,1)S(1)} %fusion.36, f32[272,1024]{1,0:T(8,128)S(1)} %get-tuple-element.112, f32[1024]{0:T(1024)S(1)} %maximum_convert_fusion.5, f32[1024]{0:T(1024)S(1)} %get-tuple-element.173, f32[272]{0:T(512)S(1)} %add_rsqrt_fusion, f32[272]{0:T(512)S(1)} %broadcast_multiply_fusion.4), kind=kOutput, calls=%fused_computation.184 | convolution fusion | flops 571817984 | bytes 5875840 | tf_op jit(solution)/shard_map/dot_general | solution.py:299
  122.7 1.4 collective-permute-start.9
  124.1 3.8 %collective-permute-done.12 = bf16[272,512]{1,0:T(8,128)(2,1)S(1)} collective-permute-done((bf16[272,512]{1,0:T(8,128)(2,1)S(1)}, bf16[272,512]{1,0:T(8,128)(2,1)S(1)}, u32[]{:S(2)}, u32[]{:S(2)}) %collective-permute-start.12) | collective-permute-done | bytes 278560 | tf_op jit(solution)/shard_map/ppermute | solution.py:276
  129.3 2.7 slice.416
  132.0 1.5 collective-permute-start.15
  134.8 1.1 fusion.40
  136.3 2.0 fusion.68
  139.5 4.7 %all-to-all-start.2 = ((bf16[4,272,64]{1,2,0:T(8,128)(2,1)}), bf16[4,272,64]{1,2,0:T(8,128)(2,1)S(1)}, u32[]{:S(2)}, u32[]{:S(2)}) async-start(bf16[4,272,64]{1,2,0:T(8,128)(2,1)} %bitcast.13), calls=%async_computation.2 | async-start | bytes 393216 | tf_op jit(solution)/shard_map/all_to_all | solution.py:438
  147.8 4.1 %all-to-all-done.2 = bf16[4,272,64]{1,2,0:T(8,128)(2,1)S(1)} async-done(((bf16[4,272,64]{1,2,0:T(8,128)(2,1)}), bf16[4,272,64]{1,2,0:T(8,128)(2,1)S(1)}, u32[]{:S(2)}, u32[]{:S(2)}) %all-to-all-start.2) | async-done | bytes 139296 | tf_op jit(solution)/shard_map/all_to_all | solution.py:438
  152.3 2.8 collective-permute-done.14
  155.1 3.2 fusion.7
  158.3 3.5 %multiply_reduce_fusion = (f32[1088]{0:T(1024)S(1)}, f32[1088,1088]{0,1:T(8,128)S(1)}) fusion(f32[1088]{0:T(1024)S(1)} %copy-done.27, f32[1088,1088]{0,1:T(8,128)} %copy-done.1, f32[1088]{0:T(1024)S(1)} %copy-done.25, bf16[1088,64]{0,1:T(8,128)(2,1)S(1)} %reshape.319, bf16[1088,256]{1,0:T(8,128)(2,1)S(1)} %bitcast.72), kind=kOutput, calls=%fused_computation.3 | convolution fusion | flops 156253120 | bytes 9916672 | tf_op jit(solution)/shard_map/dot_general | solution.py:299
  161.8 3.5 %multiply_convert_fusion = bf16[1088,1088]{0,1:T(8,128)(2,1)S(1)} fusion(f32[1088,1088]{0,1:T(8,128)S(1)} %get-tuple-element.169, f32[1088]{0:T(1024)S(1)} %get-tuple-element.168, f32[1088]{0:T(1024)S(1)} %copy-done.27, f32[1088,1088]{0,1:T(8,128)} %copy-done.1, f32[1088]{0:T(1024)S(1)} %copy-done.25), kind=kLoop, calls=%fused_computation.2 | loop fusion | flops 5918720 | bytes 11850496 | tf_op jit(solution)/shard_map/convert_element_type | solution.py:446
  165.3 3.4 convolution_convert_fusion
  168.9 1.6 fusion.4
  171.4 1.8 fusion.5
  173.4 2.0 pad_maximum_fusion.5
  175.4 4.7 %all-to-all-start.3 = ((bf16[4,272,192]{2,1,0:T(8,128)(2,1)}), bf16[4,272,192]{2,1,0:T(8,128)(2,1)S(1)}, u32[]{:S(2)}, u32[]{:S(2)}) async-start(bf16[4,272,192]{2,1,0:T(8,128)(2,1)} %pad_maximum_fusion.5), calls=%async_computation.3 | async-start | bytes 1114112 | tf_op jit(solution)/shard_map/all_to_all | solution.py:451
  181.2 3.2 fusion.6
  184.3 1.7 fusion.45
  186.1 16.8 %all-to-all-done.3 = bf16[4,272,192]{2,1,0:T(8,128)(2,1)S(1)} async-done(((bf16[4,272,192]{2,1,0:T(8,128)(2,1)}), bf16[4,272,192]{2,1,0:T(8,128)(2,1)S(1)}, u32[]{:S(2)}, u32[]{:S(2)}) %all-to-all-start.3) | async-done | bytes 417824 | tf_op jit(solution)/shard_map/all_to_all | solution.py:451
  203.3 1.2 fusion.59
  204.7 1.4 copy-done.17
  207.9 1.4 collective-permute-done.17
  209.9 8.2 %collective-permute-done.18 = bf16[272,512]{1,0:T(8,128)(2,1)S(1)} collective-permute-done((bf16[272,512]{1,0:T(8,128)(2,1)S(1)}, bf16[272,512]{1,0:T(8,128)(2,1)S(1)}, u32[]{:S(2)}, u32[]{:S(2)}) %collective-permute-start.18) | collective-permute-done | bytes 278560 | tf_op jit(solution)/shard_map/ppermute | solution.py:276
  218.3 9.5 %collective-permute-done.20 = bf16[512,768]{1,0:T(8,128)(2,1)S(1)} collective-permute-done((bf16[512,768]{1,0:T(8,128)(2,1)S(1)}, bf16[512,768]{1,0:T(8,128)(2,1)S(1)}, u32[]{:S(2)}, u32[]{:S(2)}) %collective-permute-start.20) | collective-permute-done | bytes 786464 | tf_op jit(solution)/shard_map/ppermute | solution.py:276
  227.8 1.6 fusion.8
  229.4 7.4 %all-reduce.4.cloned.1.call-done = bf16[1024,512]{1,0:T(8,128)(2,1)} async-done(((bf16[1024,512]{1,0:T(8,128)(2,1)}), bf16[1024,512]{1,0:T(8,128)(2,1)}) %all-reduce.4.cloned.1.call-update) | async-done | bytes 1048592 | tf_op jit(solution)/shard_map/psum | solution.py:442
  236.8 1.2 copy.63
  238.1 1.6 convert_element_type.314
  239.8 1.1 broadcast_select_fusion.1
  241.7 1.5 collective-permute-start.21
  243.7 1.8 collective-permute-done.21
  245.5 1.3 collective-permute-start.22
  246.9 2.6 collective-permute-done.22
  249.5 1.6 collective-permute-start.23
  251.2 1.2 fusion.42
  252.4 2.2 collective-permute-done.23
  255.9 72.0 %all-reduce.6.cloned.1.call-done = (bf16[512,3,256]{0,2,1:T(8,128)(2,1)}, bf16[256,512]{1,0:T(8,128)(2,1)}, bf16[512,1024]{1,0:T(8,128)(2,1)}) async-done(((bf16[512,3,256]{0,2,1:T(8,128)(2,1)}, bf16[256,512]{1,0:T(8,128)(2,1)}, bf16[512,1024]{1,0:T(8,128)(2,1)}), (bf16[512,3,256]{0,2,1:T(8,128)(2,1)}, bf16[256,512]{1,0:T(8,128)(2,1)}, bf16[512,1024]{1,0:T(8,128)(2,1)})) %all-reduce.6.cloned.1.call-update) | async-done | bytes 2097168 | tf_op jit(solution)/shard_map/psum | solution.py:460
  327.9 1.9 convert_element_type.312
  329.8 1.4 copy.64
  331.2 1.6 convert_element_type.313
  (245 shorter events, 39.6 us)
Async XLA Ops:
  7.2 11.5 %copy-start.13 = (bf16[1,272,1024]{2,1,0:T(8,128)(2,1)S(1)}, bf16[1,272,1024]{2,1,0:T(8,128)(2,1)}, u32[]{:S(2)}) copy-start(bf16[1,272,1024]{2,1,0:T(8,128)(2,1)} %param.15) | copy-start | bytes 1671172
  14.2 5.3 %collective-permute-start = (bf16[3840]{0:T(1024)(128)(2,1)S(1)}, bf16[3840]{0:T(1024)(128)(2,1)S(1)}, u32[]{:S(2)}, u32[]{:S(2)}) collective-permute-start(bf16[3840]{0:T(1024)(128)(2,1)S(1)} %dynamic-update-slice.31), channel_id=1, source_target_pairs={{0,16},{16,0},{1,17},{17,1},{2,18},{18,2},{3,19},{19,3},{4,20},{20... | collective-permute-start | bytes 23048 | tf_op jit(solution)/shard_map/ppermute | solution.py:276
  18.6 19.1 %copy-start.16 = (bf16[512,3,256]{0,2,1:T(8,128)(2,1)}, bf16[512,3,256]{0,2,1:T(8,128)(2,1)S(1)}, u32[]{:S(2)}) copy-start(bf16[512,3,256]{0,2,1:T(8,128)(2,1)S(1)} %copy.51) | copy-start | bytes 2359300
  18.6 19.1 %collective-permute-start.1 = (bf16[512,768]{0,1:T(8,128)(2,1)S(1)}, bf16[512,768]{0,1:T(8,128)(2,1)S(1)}, u32[]{:S(2)}, u32[]{:S(2)}) collective-permute-start(bf16[512,768]{0,1:T(8,128)(2,1)S(1)} %bitcast.84), channel_id=1, source_target_pairs={{0,16},{16,0},{1,17},{17,1},{2,18},{18,2},{3,19},{19,3},{4,20},{20... | collective-permute-start | bytes 2359304 | tf_op jit(solution)/shard_map/ppermute | solution.py:276
  19.5 18.9 %copy-start.22 = (f32[272]{0:T(512)}, f32[272]{0:T(512)S(1)}, u32[]{:S(2)}) copy-start(f32[272]{0:T(512)S(1)} %add_rsqrt_fusion.1) | copy-start | bytes 3268
  19.9 18.5 %copy-start.28 = (f32[1024]{0:T(1024)}, f32[1024]{0:T(1024)S(1)}, u32[]{:S(2)}) copy-start(f32[1024]{0:T(1024)S(1)} %get-tuple-element.171) | copy-start | bytes 12292
  39.1 6.0 %copy-start.12 = (bf16[1,272,1024]{2,1,0:T(8,128)(2,1)S(1)}, bf16[1,272,1024]{2,1,0:T(8,128)(2,1)}, u32[]{:S(2)}) copy-start(bf16[1,272,1024]{2,1,0:T(8,128)(2,1)} %param.17) | copy-start | bytes 1671172
  40.2 18.9 %all-to-all-start = ((bf16[4,272,256]{2,1,0:T(8,128)(2,1)}), bf16[4,272,256]{2,1,0:T(8,128)(2,1)S(1)}, u32[]{:S(2)}, u32[]{:S(2)}) async-start(bf16[4,272,256]{2,1,0:T(8,128)(2,1)} %copy.54), calls=%async_computation | async-start | bytes 1114112 | tf_op jit(solution)/shard_map/all_to_all | solution.py:386
  45.3 24.0 %collective-permute-start.3 = (bf16[256,512]{1,0:T(8,128)(2,1)}, bf16[256,512]{1,0:T(8,128)(2,1)}, u32[]{:S(2)}, u32[]{:S(2)}) collective-permute-start(bf16[256,512]{1,0:T(8,128)(2,1)} %param.20), channel_id=1, source_target_pairs={{0,16},{16,0},{1,17},{17,1},{2,18},{18,2},{3,19},{19,3},{4,20},{20... | collective-permute-start | bytes 786440 | tf_op jit(solution)/shard_map/ppermute | solution.py:276
  45.9 28.9 %collective-permute-start.2 = (bf16[512,1024]{1,0:T(8,128)(2,1)}, bf16[512,1024]{1,0:T(8,128)(2,1)S(1)}, u32[]{:S(2)}, u32[]{:S(2)}) collective-permute-start(bf16[512,1024]{1,0:T(8,128)(2,1)} %param.22), channel_id=1, source_target_pairs={{0,16},{16,0},{1,17},{17,1},{2,18},{18,2},{3,19},{19,3},{4,20},{20... | collective-permute-start | bytes 3145736 | tf_op jit(solution)/shard_map/ppermute | solution.py:276
  59.1 2.2 copy-start.6
  60.5 2.3 copy-start.1
  60.5 2.3 copy-start.24
  64.7 10.0 %all-to-all-start.1 = ((bf16[4,272,64]{1,2,0:T(8,128)(2,1)}), bf16[4,272,64]{1,2,0:T(8,128)(2,1)S(1)}, u32[]{:S(2)}, u32[]{:S(2)}) async-start(bf16[4,272,64]{1,2,0:T(8,128)(2,1)} %copy.55), calls=%async_computation.1 | async-start | bytes 393216 | tf_op jit(solution)/shard_map/all_to_all | solution.py:401
  70.3 7.9 %copy-start.8 = (bf16[256,1024]{1,0:T(8,128)(2,1)}, bf16[256,1024]{1,0:T(8,128)(2,1)S(1)}, u32[]{:S(2)}) copy-start(bf16[256,1024]{1,0:T(8,128)(2,1)S(1)} %constant_dynamic-update-slice_fusion) | copy-start | bytes 1572868
  75.9 3.6 %collective-permute-start.4 = (bf16[272,512]{1,0:T(8,128)(2,1)}, bf16[272,512]{1,0:T(8,128)(2,1)}, u32[]{:S(2)}, u32[]{:S(2)}) collective-permute-start(bf16[272,512]{1,0:T(8,128)(2,1)} %broadcast_select_fusion.11), channel_id=1, source_target_pairs={{0,1},{1,0},{2,3},{3,2},{4,5},{5,4},{6,7},{7,6},{8,9},{9,8},{10,11... | collective-permute-start | bytes 835592 | tf_op jit(solution)/shard_map/ppermute | solution.py:276
  79.4 4.1 %copy-start.41 = (bf16[512]{0:T(512)(128)(2,1)S(1)}, bf16[512]{0:T(512)(128)(2,1)}, u32[]{:S(2)}) copy-start(bf16[512]{0:T(512)(128)(2,1)} %param.25) | copy-start | bytes 3076
  80.5 4.1 %copy-start.42 = (bf16[512]{0:T(512)(128)(2,1)S(1)}, bf16[512]{0:T(512)(128)(2,1)}, u32[]{:S(2)}) copy-start(bf16[512]{0:T(512)(128)(2,1)} %param.29) | copy-start | bytes 3076
  80.5 9.3 %copy-start.43 = (bf16[4,128]{1,0:T(4,128)(2,1)S(1)}, bf16[4,128]{1,0:T(4,128)(2,1)}, u32[]{:S(2)}) copy-start(bf16[4,128]{1,0:T(4,128)(2,1)} %param.23) | copy-start | bytes 3076
  80.5 9.4 %copy-start.39 = (bf16[512]{0:T(512)(128)(2,1)S(1)}, bf16[512]{0:T(512)(128)(2,1)}, u32[]{:S(2)}) copy-start(bf16[512]{0:T(512)(128)(2,1)} %param.28) | copy-start | bytes 3076
  80.6 9.4 %copy-start.40 = (bf16[512]{0:T(512)(128)(2,1)S(1)}, bf16[512]{0:T(512)(128)(2,1)}, u32[]{:S(2)}) copy-start(bf16[512]{0:T(512)(128)(2,1)} %param.21) | copy-start | bytes 3076
  80.6 9.4 %copy-start.19 = (bf16[1024,1024]{1,0:T(8,128)(2,1)S(1)}, bf16[1024,1024]{1,0:T(8,128)(2,1)}, u32[]{:S(2)}) copy-start(bf16[1024,1024]{1,0:T(8,128)(2,1)} %constant_dynamic-update-slice_fusion.3) | copy-start | bytes 6291460
  80.6 9.1 %collective-permute-start.5 = (bf16[272,512]{1,0:T(8,128)(2,1)S(1)}, bf16[272,512]{1,0:T(8,128)(2,1)S(1)}, u32[]{:S(2)}, u32[]{:S(2)}) collective-permute-start(bf16[272,512]{1,0:T(8,128)(2,1)S(1)} %add_convert_fusion.9), channel_id=1, source_target_pairs={{0,2},{1,3},{2,0},{3,1},{4,6},{5,7},{6,4},{7,5},{8,10},{9,11},{10,... | collective-permute-start | bytes 835592 | tf_op jit(solution)/shard_map/ppermute | solution.py:276
  84.1 25.5 %collective-permute-start.7 = (bf16[1024,512]{1,0:T(8,128)(2,1)}, bf16[1024,512]{1,0:T(8,128)(2,1)S(1)}, u32[]{:S(2)}, u32[]{:S(2)}) collective-permute-start(bf16[1024,512]{1,0:T(8,128)(2,1)} %param.24), channel_id=1, source_target_pairs={{0,16},{16,0},{1,17},{17,1},{2,18},{18,2},{3,19},{19,3},{4,20},{20... | collective-permute-start | bytes 3145736 | tf_op jit(solution)/shard_map/ppermute | solution.py:276
  89.8 1.6 collective-permute-start.6
  110.2 9.0 %copy-start.20 = (f32[272]{0:T(512)}, f32[272]{0:T(512)S(1)}, u32[]{:S(2)}) copy-start(f32[272]{0:T(512)S(1)} %add_rsqrt_fusion) | copy-start | bytes 3268
  112.6 2.1 copy-start
  116.7 1.6 collective-permute-start.11
  117.7 5.0 %collective-permute-start.8 = (bf16[272,512]{1,0:T(8,128)(2,1)S(1)}, bf16[272,512]{1,0:T(8,128)(2,1)S(1)}, u32[]{:S(2)}, u32[]{:S(2)}) collective-permute-start(bf16[272,512]{1,0:T(8,128)(2,1)S(1)} %broadcast_select_fusion.8), channel_id=1, source_target_pairs={{0,1},{1,0},{2,3},{3,2},{4,5},{5,4},{6,7},{7,6},{8,9},{9,8},{10,11... | collective-permute-start | bytes 835592 | tf_op jit(solution)/shard_map/ppermute | solution.py:276
  118.4 9.6 %collective-permute-start.12 = (bf16[272,512]{1,0:T(8,128)(2,1)S(1)}, bf16[272,512]{1,0:T(8,128)(2,1)S(1)}, u32[]{:S(2)}, u32[]{:S(2)}) collective-permute-start(bf16[272,512]{1,0:T(8,128)(2,1)S(1)} %add_convert_fusion.5), channel_id=1, source_target_pairs={{0,2},{1,3},{2,0},{3,1},{4,6},{5,7},{6,4},{7,5},{8,10},{9,11},{10,... | collective-permute-start | bytes 835592 | tf_op jit(solution)/shard_map/ppermute | solution.py:276
  122.7 10.8 %collective-permute-start.9 = (bf16[272,512]{1,0:T(8,128)(2,1)S(1)}, bf16[272,512]{1,0:T(8,128)(2,1)}, u32[]{:S(2)}, u32[]{:S(2)}) collective-permute-start(bf16[272,512]{1,0:T(8,128)(2,1)S(1)} %add_convert_fusion.7), channel_id=1, source_target_pairs={{0,2},{1,3},{2,0},{3,1},{4,6},{5,7},{6,4},{7,5},{8,10},{9,11},{10,... | collective-permute-start | bytes 835592 | tf_op jit(solution)/shard_map/ppermute | solution.py:276
  128.0 6.6 %collective-permute-start.13 = (bf16[272,512]{1,0:T(8,128)(2,1)S(1)}, bf16[272,512]{1,0:T(8,128)(2,1)S(1)}, u32[]{:S(2)}, u32[]{:S(2)}) collective-permute-start(bf16[272,512]{1,0:T(8,128)(2,1)S(1)} %add_convert_fusion.4), channel_id=1, source_target_pairs={{0,1},{1,0},{2,3},{3,2},{4,5},{5,4},{6,7},{7,6},{8,9},{9,8},{10,11... | collective-permute-start | bytes 835592 | tf_op jit(solution)/shard_map/ppermute | solution.py:276
  128.8 26.3 %collective-permute-start.14 = (bf16[1024,512]{1,0:T(8,128)(2,1)}, bf16[1024,512]{1,0:T(8,128)(2,1)}, u32[]{:S(2)}, u32[]{:S(2)}) collective-permute-start(bf16[1024,512]{1,0:T(8,128)(2,1)} %slice.417), channel_id=1, source_target_pairs={{0,16},{16,0},{1,17},{17,1},{2,18},{18,2},{3,19},{19,3},{4,20},{20... | collective-permute-start | bytes 3145736 | tf_op jit(solution)/shard_map/ppermute | solution.py:276
  132.0 2.7 copy-start.21
  132.0 49.1 %collective-permute-start.15 = (bf16[512,1024]{1,0:T(8,128)(2,1)}, bf16[512,1024]{1,0:T(8,128)(2,1)}, u32[]{:S(2)}, u32[]{:S(2)}) collective-permute-start(bf16[512,1024]{1,0:T(8,128)(2,1)} %slice.416), channel_id=1, source_target_pairs={{0,16},{16,0},{1,17},{17,1},{2,18},{18,2},{3,19},{19,3},{4,20},{20... | collective-permute-start | bytes 3145736 | tf_op jit(solution)/shard_map/ppermute | solution.py:276
  134.6 1.6 collective-permute-start.10
  136.3 2.0 copy-start.9
  138.3 5.9 %copy-start.2 = (f32[272,1024]{1,0:T(8,128)}, f32[272,1024]{1,0:T(8,128)S(1)}, u32[]{:S(2)}) copy-start(f32[272,1024]{1,0:T(8,128)S(1)} %get-tuple-element.108) | copy-start | bytes 3342340
  139.5 12.5 %all-to-all-start.2 = ((bf16[4,272,64]{1,2,0:T(8,128)(2,1)}), bf16[4,272,64]{1,2,0:T(8,128)(2,1)S(1)}, u32[]{:S(2)}, u32[]{:S(2)}) async-start(bf16[4,272,64]{1,2,0:T(8,128)(2,1)} %bitcast.13), calls=%async_computation.2 | async-start | bytes 393216 | tf_op jit(solution)/shard_map/all_to_all | solution.py:438
  144.1 2.7 copy-start.5
  146.3 38.0 %collective-permute-start.16 = (bf16[256,512]{1,0:T(8,128)(2,1)}, bf16[256,512]{1,0:T(8,128)(2,1)}, u32[]{:S(2)}, u32[]{:S(2)}) collective-permute-start(bf16[256,512]{1,0:T(8,128)(2,1)} %slice.419), channel_id=1, source_target_pairs={{0,16},{16,0},{1,17},{17,1},{2,18},{18,2},{3,19},{19,3},{4,20},{20... | collective-permute-start | bytes 786440 | tf_op jit(solution)/shard_map/ppermute | solution.py:276
  152.3 6.0 %copy-start.7 = (bf16[4,272,256]{2,1,0:T(8,128)(2,1)S(1)}, bf16[4,272,256]{2,1,0:T(8,128)(2,1)}, u32[]{:S(2)}) copy-start(bf16[4,272,256]{2,1,0:T(8,128)(2,1)} %copy-done.6) | copy-start | bytes 1671172
  152.3 6.0 %copy-start.25 = (f32[1088]{0:T(1024)S(1)}, f32[1088]{0:T(1024)}, u32[]{:S(2)}) copy-start(f32[1088]{0:T(1024)} %copy-done.24) | copy-start | bytes 13060
  152.3 6.0 %copy-start.27 = (f32[1088]{0:T(1024)S(1)}, f32[1088]{0:T(1024)}, u32[]{:S(2)}) copy-start(f32[1088]{0:T(1024)} %copy-done.26) | copy-start | bytes 13060
  173.4 6.7 %copy-start.33 = (f32[1024]{0:T(1024)S(1)}, f32[1024]{0:T(1024)}, u32[]{:S(2)}) copy-start(f32[1024]{0:T(1024)} %get-tuple-element.107) | copy-start | bytes 12292
  173.4 6.7 %copy-start.34 = (f32[3840]{0:T(1024)S(1)}, f32[3840]{0:T(1024)}, u32[]{:S(2)}) copy-start(f32[3840]{0:T(1024)} %get-tuple-element.161) | copy-start | bytes 46084
  173.4 6.7 %copy-start.47 = (f32[3840]{0:T(1024)S(1)}, f32[3840]{0:T(1024)}, u32[]{:S(2)}) copy-start(f32[3840]{0:T(1024)} %get-tuple-element.160) | copy-start | bytes 46084
  175.4 27.4 %all-to-all-start.3 = ((bf16[4,272,192]{2,1,0:T(8,128)(2,1)}), bf16[4,272,192]{2,1,0:T(8,128)(2,1)S(1)}, u32[]{:S(2)}, u32[]{:S(2)}) async-start(bf16[4,272,192]{2,1,0:T(8,128)(2,1)} %pad_maximum_fusion.5), calls=%async_computation.3 | async-start | bytes 1114112 | tf_op jit(solution)/shard_map/all_to_all | solution.py:451
  180.1 56.7 %all-reduce.4.cloned.1.call-start = ((), (), s32[]{:S(2)}) async-start(), calls=%async_computation.4 | async-start | bytes 2097152 | tf_op jit(solution)/shard_map/psum | solution.py:442
  180.8 3.5 %copy-start.11 = (f32[256,1024]{1,0:T(8,128)S(1)}, f32[256,1024]{1,0:T(8,128)}, u32[]{:S(2)}) copy-start(f32[256,1024]{1,0:T(8,128)} %copy-done.10) | copy-start | bytes 3145732
  180.8 147.1 %all-reduce.6.cloned.1.call-start = ((), (), s32[]{:S(2)}) async-start(), calls=%async_computation.5 | async-start | bytes 4194304 | tf_op jit(solution)/shard_map/psum | solution.py:460
  186.1 17.2 %copy-start.23 = (f32[272]{0:T(512)S(1)}, f32[272]{0:T(512)}, u32[]{:S(2)}) copy-start(f32[272]{0:T(512)} %copy-done.22) | copy-start | bytes 3268
  186.1 17.2 %copy-start.29 = (f32[1024]{0:T(1024)S(1)}, f32[1024]{0:T(1024)}, u32[]{:S(2)}) copy-start(f32[1024]{0:T(1024)} %copy-done.28) | copy-start | bytes 12292
  204.4 3.2 copy-start.4
  204.4 2.5 copy-start.46
  207.6 1.6 collective-permute-start.17
  207.9 19.9 %collective-permute-start.20 = (bf16[512,768]{1,0:T(8,128)(2,1)S(1)}, bf16[512,768]{1,0:T(8,128)(2,1)S(1)}, u32[]{:S(2)}, u32[]{:S(2)}) collective-permute-start(bf16[512,768]{1,0:T(8,128)(2,1)S(1)} %slice.418), channel_id=1, source_target_pairs={{0,16},{16,0},{1,17},{17,1},{2,18},{18,2},{3,19},{19,3},{4,20},{20... | collective-permute-start | bytes 2359304 | tf_op jit(solution)/shard_map/ppermute | solution.py:276
  209.4 8.8 %collective-permute-start.18 = (bf16[272,512]{1,0:T(8,128)(2,1)S(1)}, bf16[272,512]{1,0:T(8,128)(2,1)S(1)}, u32[]{:S(2)}, u32[]{:S(2)}) collective-permute-start(bf16[272,512]{1,0:T(8,128)(2,1)S(1)} %add_convert_fusion.3), channel_id=1, source_target_pairs={{0,2},{1,3},{2,0},{3,1},{4,6},{5,7},{6,4},{7,5},{8,10},{9,11},{10,... | collective-permute-start | bytes 835592 | tf_op jit(solution)/shard_map/ppermute | solution.py:276
  218.2 21.6 %collective-permute-start.19 = (bf16[272,512]{1,0:T(8,128)(2,1)S(1)}, bf16[272,512]{1,0:T(8,128)(2,1)}, u32[]{:S(2)}, u32[]{:S(2)}) collective-permute-start(bf16[272,512]{1,0:T(8,128)(2,1)S(1)} %add_convert_fusion.2), channel_id=1, source_target_pairs={{0,1},{1,0},{2,3},{3,2},{4,5},{5,4},{6,7},{7,6},{8,9},{9,8},{10,11... | collective-permute-start | bytes 835592 | tf_op jit(solution)/shard_map/ppermute | solution.py:276
  239.8 3.4 %copy-start.3 = (f32[272,1024]{1,0:T(8,128)S(1)}, f32[272,1024]{1,0:T(8,128)}, u32[]{:S(2)}) copy-start(f32[272,1024]{1,0:T(8,128)} %copy-done.2) | copy-start | bytes 3342340
  241.7 3.8 %collective-permute-start.21 = (f32[3840]{0:T(1024)S(1)}, f32[3840]{0:T(1024)S(1)}, u32[]{:S(2)}, u32[]{:S(2)}) collective-permute-start(f32[3840]{0:T(1024)S(1)} %get-tuple-element.146), channel_id=1, source_target_pairs={{0,16},{16,0},{1,17},{17,1},{2,18},{18,2},{3,19},{19,3},{4,20},{20... | collective-permute-start | bytes 46088 | tf_op jit(solution)/shard_map/ppermute | solution.py:276
  245.5 4.1 %collective-permute-start.22 = (f32[3840]{0:T(1024)S(1)}, f32[3840]{0:T(1024)S(1)}, u32[]{:S(2)}, u32[]{:S(2)}) collective-permute-start(f32[3840]{0:T(1024)S(1)} %add.176), channel_id=1, source_target_pairs={{0,4},{4,0},{8,12},{12,8},{1,5},{5,1},{9,13},{13,9},{2,6},{6,2},{1... | collective-permute-start | bytes 46088 | tf_op jit(solution)/shard_map/ppermute | solution.py:276
  249.5 5.1 %collective-permute-start.23 = (f32[3840]{0:T(1024)S(1)}, f32[3840]{0:T(1024)S(1)}, u32[]{:S(2)}, u32[]{:S(2)}) collective-permute-start(f32[3840]{0:T(1024)S(1)} %add.177), channel_id=1, source_target_pairs={{0,8},{4,12},{8,0},{12,4},{1,9},{5,13},{9,1},{13,5},{2,10},{6,14},... | collective-permute-start | bytes 46088 | tf_op jit(solution)/shard_map/ppermute | solution.py:276
  327.9 1.9 copy-start.18
  (14 other events, 18.1 us)
Sparse Core Ops, SparseCore 0:
  183.3 53.5 all-reduce.3
  240.1 87.7 all-reduce.5
